TPU v7x, 32 devices: a whole 2x2x4 slice. The times are simulated.
32 devices in a mesh: dp: 8 (over z, core), seq: 4 (over y, x).
Axes of the slice: x: 2, y: 2, z: 4, core: 2. Of those that a mesh axis runs over, the one named last changes fastest.
Arguments:
- tokens: bfloat16 [8, 2048, 1024], P('dp', 'seq'), may hold values from -6 to 6
- input_weight: bfloat16 [1024, 3072], P(('dp', 'seq')), may hold values from -0.1875 to 0.1875
- input_bias: bfloat16 [3072], P(('dp', 'seq')), may hold values from -1.75 to 1.75
- output_weight: bfloat16 [1024, 1024], P(('dp', 'seq')), may hold values from -4 to 4
- output_bias: bfloat16 [1024], P(('dp', 'seq')), may hold values from -1.75 to 1.75
- up_weight: bfloat16 [1024, 4096], P(('dp', 'seq')), may hold values from -0.1875 to 0.1875
- up_bias: bfloat16 [4096], P(('dp', 'seq')), may hold values from -1.75 to 1.75
- down_weight: bfloat16 [4096, 1024], P(('dp', 'seq')), may hold values from -0.09375 to 0.09375
- down_bias: bfloat16 [1024], P(('dp', 'seq')), may hold values from -1.75 to 1.75
- attention_gain: bfloat16 [1024], P(('dp', 'seq')), may hold values from 0.099609375 to 1.8984375
- attention_shift: bfloat16 [1024], P(('dp', 'seq')), may hold values from -1.75 to 1.75
- feedforward_gain: bfloat16 [1024], P(('dp', 'seq')), may hold values from 0.099609375 to 1.8984375
- feedforward_shift: bfloat16 [1024], P(('dp', 'seq')), may hold values from -1.75 to 1.75
- cotangent: bfloat16 [8, 2048, 1024], P('dp', 'seq'), may hold values from -6 to 6
Outputs:
- output: bfloat16 [8, 2048, 1024], P('dp', 'seq')
- token_grad: bfloat16 [8, 2048, 1024], P('dp', 'seq')
- input_weight_grad: float32 [1024, 3072], P(('dp', 'seq'))
- input_bias_grad: float32 [2048], P(('dp', 'seq'))
- value_bias_grad: float32 [1024], P(('dp', 'seq'))
- output_weight_grad: float32 [1024, 1024], P(('dp', 'seq'))
- output_bias_grad: float32 [1024], P(('dp', 'seq'))
- up_weight_grad: float32 [1024, 4096], P(('dp', 'seq'))
- up_bias_grad: float32 [4096], P(('dp', 'seq'))
- down_weight_grad: float32 [4096, 1024], P(('dp', 'seq'))
- down_bias_grad: float32 [1024], P(('dp', 'seq'))
- attention_gain_grad: float32 [1024], P(('dp', 'seq'))
- attention_shift_grad: float32 [1024], P(('dp', 'seq'))
- feedforward_gain_grad: float32 [1024], P(('dp', 'seq'))
- feedforward_shift_grad: float32 [1024], P(('dp', 'seq'))
All inputs are finite; a program needn't handle non-finite values.
Results may differ from a plain program's by a relative error of at most 0.014.
Values may be sent and summed in bfloat16 or wider, within the bound.
No kernel may reach another device: no remote copies, remote signals or barrier semaphores. Data moves between devices by JAX's collectives and lax.ppermute only.
A program may use at most 256 MiB of HBM per device.

v0:
```python
import math

import jax
import jax.numpy as jnp
from jax import lax
from jax.sharding import PartitionSpec as P

HEADS = 16
ROT = 16


norm_eps = 1e-05
masked_score = -1e30


def layer_norm(inputs, gain, shift):
    centered = inputs - jnp.mean(inputs, axis=-1, keepdims=True)
    variance = jnp.mean(centered * centered, axis=-1, keepdims=True)
    return centered * lax.rsqrt(variance + norm_eps) * gain + shift


def exact_gelu(inputs):
    return jax.nn.gelu(inputs, approximate=False)


def rotary_tables(positions, rotary_dims):
    exponent = -jnp.arange(0, rotary_dims, 2, dtype=jnp.float32) / rotary_dims
    frequency = jnp.float32(10000.0) ** exponent
    phase = positions.astype(jnp.float32)[:, None] * frequency[None, :]
    phase = jnp.concatenate([phase, phase], axis=-1)
    return (jnp.cos(phase), jnp.sin(phase))


def rotate(inputs, cosine, sine):
    rotary_dims = cosine.shape[-1]
    half = rotary_dims // 2
    front = inputs[..., :rotary_dims]
    turned = jnp.concatenate([-front[..., half:], front[..., :half]], axis=-1)
    front = front * cosine[:, None, :] + turned * sine[:, None, :]
    return jnp.concatenate([front, inputs[..., rotary_dims:]], axis=-1)


def rounded(inputs):
    return lax.optimization_barrier(inputs.astype(jnp.bfloat16)).astype(jnp.float32)


def attend_block(query_block, query_pos, key_block, value_block, key_pos, running, scale):
    running_max, running_total, running_sum = running
    scores = (
        jnp.einsum("sqhe,skhe->shqk", query_block, key_block, preferred_element_type=jnp.float32)
        * scale
    )
    allowed = key_pos[None, None, None, :] <= query_pos[None, None, :, None]
    scores = jnp.where(allowed, scores, masked_score)
    new_max = jnp.maximum(running_max, jnp.max(scores, axis=-1))
    factor = jnp.exp(running_max - new_max)
    weights = jnp.where(allowed, jnp.exp(scores - new_max[..., None]), 0.0)
    running_total = running_total * factor + jnp.sum(weights, axis=-1)
    update = jnp.einsum(
        "shqk,skhe->sqhe",
        weights.astype(jnp.bfloat16),
        value_block,
        preferred_element_type=jnp.float32,
    )
    running_sum = running_sum * jnp.swapaxes(factor, 1, 2)[..., None] + update
    return (new_max, running_total, running_sum)


def score_parts(
    query_block, query_pos, grad_block, logsum, delta, key_block, value_block, key_pos, scale
):
    scores = (
        jnp.einsum("sqhe,skhe->shqk", query_block, key_block, preferred_element_type=jnp.float32)
        * scale
    )
    allowed = key_pos[None, None, None, :] <= query_pos[None, None, :, None]
    probs = jnp.where(allowed, jnp.exp(scores - logsum[..., None]), 0.0)
    prob_grad = jnp.einsum(
        "sqhe,skhe->shqk", grad_block, value_block, preferred_element_type=jnp.float32
    )
    score_grad = (probs * (prob_grad - delta[..., None])).astype(jnp.bfloat16)
    return (probs.astype(jnp.bfloat16), score_grad)


def split_blocks(piece, block):
    seqs = piece.shape[0]
    blocks = piece.shape[1] // block
    return jnp.moveaxis(piece.reshape(seqs, blocks, block, HEADS, piece.shape[2] // HEADS), 1, 0)


def on_device(
    tokens,
    input_weight,
    input_bias,
    output_weight,
    output_bias,
    up_weight,
    up_bias,
    down_weight,
    down_bias,
    attention_gain,
    attention_shift,
    feedforward_gain,
    feedforward_shift,
    cotangent,
):
    gathered = (
        lax.all_gather(input_weight, ("dp", "seq"), axis=0, tiled=True),
        lax.all_gather(input_bias, ("dp", "seq"), axis=0, tiled=True),
        lax.all_gather(output_weight, ("dp", "seq"), axis=0, tiled=True),
        lax.all_gather(output_bias, ("dp", "seq"), axis=0, tiled=True),
        lax.all_gather(up_weight, ("dp", "seq"), axis=0, tiled=True),
        lax.all_gather(up_bias, ("dp", "seq"), axis=0, tiled=True),
        lax.all_gather(down_weight, ("dp", "seq"), axis=0, tiled=True),
        lax.all_gather(down_bias, ("dp", "seq"), axis=0, tiled=True),
        lax.all_gather(attention_gain, ("dp", "seq"), axis=0, tiled=True),
        lax.all_gather(attention_shift, ("dp", "seq"), axis=0, tiled=True),
        lax.all_gather(feedforward_gain, ("dp", "seq"), axis=0, tiled=True),
        lax.all_gather(feedforward_shift, ("dp", "seq"), axis=0, tiled=True),
    )
    seqs = tokens.shape[0]
    block = tokens.shape[1]
    width = tokens.shape[2]
    rows = seqs * block
    head_dim = width // HEADS
    scale = 1.0 / math.sqrt(head_dim)
    seq_count = lax.axis_size("seq")
    seq_place = lax.axis_index("seq")
    first_row = seq_place * block
    row_steps = jnp.arange(block, dtype=jnp.int32)
    query_pos = first_row + row_steps
    cosine, sine = rotary_tables(query_pos, ROT)
    floats = tokens.reshape(rows, width).astype(jnp.float32)
    attn_gain = gathered[8].astype(jnp.float32)
    attn_shift = gathered[9].astype(jnp.float32)
    ff_gain = gathered[10].astype(jnp.float32)
    ff_shift = gathered[11].astype(jnp.float32)
    normed_attn = layer_norm(floats, attn_gain, attn_shift).astype(jnp.bfloat16)
    mixed = jnp.dot(normed_attn, gathered[0], preferred_element_type=jnp.float32) + gathered[
        1
    ].astype(jnp.float32)
    query_rot = rotate(mixed[:, :width].reshape(seqs, block, HEADS, head_dim), cosine, sine).astype(
        jnp.bfloat16
    )
    key_rot = rotate(
        mixed[:, width : 2 * width].reshape(seqs, block, HEADS, head_dim), cosine, sine
    ).astype(jnp.bfloat16)
    value_part = mixed[:, 2 * width :].astype(jnp.bfloat16).reshape(seqs, block, width)
    key_flat = key_rot.reshape(seqs, block, width)
    start_state = (
        jnp.full((seqs, HEADS, block), masked_score, jnp.float32),
        jnp.zeros((seqs, HEADS, block), jnp.float32),
        jnp.zeros((seqs, block, HEADS, head_dim), jnp.float32),
    )
    running = start_state
    key_blocks = split_blocks(lax.all_gather(key_flat, "seq", axis=1, tiled=True), block)
    value_blocks = split_blocks(lax.all_gather(value_part, "seq", axis=1, tiled=True), block)
    count = key_blocks.shape[0]

    def visit(state, item):
        number, key_block, value_block = item
        block_start = number * block
        key_pos = block_start + row_steps

        def attend(kept):
            return attend_block(query_rot, query_pos, key_block, value_block, key_pos, kept, scale)

        return (lax.cond(block_start < first_row + block, attend, lambda kept: kept, state), None)

    running, _ = lax.scan(
        visit, running, (jnp.arange(count, dtype=jnp.int32), key_blocks, value_blocks)
    )
    running_max, running_total, running_sum = running
    logsum = running_max + jnp.log(running_total)
    attended = running_sum / jnp.swapaxes(running_total, 1, 2)[..., None]
    attended_low = attended.reshape(rows, width).astype(jnp.bfloat16)
    attention_out = jnp.dot(
        attended_low, gathered[2], preferred_element_type=jnp.float32
    ) + gathered[3].astype(jnp.float32)
    normed_ff = layer_norm(floats, ff_gain, ff_shift).astype(jnp.bfloat16)
    hidden = jnp.dot(normed_ff, gathered[4], preferred_element_type=jnp.float32) + gathered[
        5
    ].astype(jnp.float32)
    active, gelu_pull = jax.vjp(exact_gelu, hidden)
    active_low = active.astype(jnp.bfloat16)
    ff_out = jnp.dot(active_low, gathered[6], preferred_element_type=jnp.float32) + gathered[
        7
    ].astype(jnp.float32)
    output = (floats + attention_out + ff_out).astype(jnp.bfloat16).reshape(seqs, block, width)
    backward_weights = (
        lax.all_gather(input_weight, ("dp", "seq"), axis=0, tiled=True),
        lax.all_gather(input_bias, ("dp", "seq"), axis=0, tiled=True),
        lax.all_gather(output_weight, ("dp", "seq"), axis=0, tiled=True),
        lax.all_gather(output_bias, ("dp", "seq"), axis=0, tiled=True),
        lax.all_gather(up_weight, ("dp", "seq"), axis=0, tiled=True),
        lax.all_gather(up_bias, ("dp", "seq"), axis=0, tiled=True),
        lax.all_gather(down_weight, ("dp", "seq"), axis=0, tiled=True),
        lax.all_gather(down_bias, ("dp", "seq"), axis=0, tiled=True),
        lax.all_gather(attention_gain, ("dp", "seq"), axis=0, tiled=True),
        lax.all_gather(attention_shift, ("dp", "seq"), axis=0, tiled=True),
        lax.all_gather(feedforward_gain, ("dp", "seq"), axis=0, tiled=True),
        lax.all_gather(feedforward_shift, ("dp", "seq"), axis=0, tiled=True),
    )
    cot_rows = cotangent.reshape(rows, width)
    grad_out = cot_rows.astype(jnp.float32)
    out_weight_grad = jnp.dot(attended_low.T, cot_rows, preferred_element_type=jnp.float32)
    out_bias_grad = jnp.sum(grad_out, axis=0)
    down_weight_grad = jnp.dot(active_low.T, cot_rows, preferred_element_type=jnp.float32)
    attended_grad = jnp.dot(
        cot_rows, backward_weights[2].T, preferred_element_type=jnp.float32
    ).astype(jnp.bfloat16)
    active_grad = jnp.dot(cot_rows, backward_weights[6].T, preferred_element_type=jnp.float32)
    hidden_grad = gelu_pull(active_grad)[0].astype(jnp.bfloat16)
    up_weight_grad = jnp.dot(normed_ff.T, hidden_grad, preferred_element_type=jnp.float32)
    up_bias_grad = jnp.sum(hidden_grad.astype(jnp.float32), axis=0)
    normed_ff_grad = jnp.dot(hidden_grad, backward_weights[4].T, preferred_element_type=jnp.float32)
    attended_heads_grad = attended_grad.reshape(seqs, block, HEADS, head_dim)
    delta = jnp.swapaxes(jnp.sum(attended_heads_grad.astype(jnp.float32) * attended, axis=-1), 1, 2)
    zero_heads = jnp.zeros((seqs, block, HEADS, head_dim), jnp.float32)
    key_all, value_all = (
        lax.all_gather(key_flat, "seq", axis=1, tiled=True),
        lax.all_gather(value_part, "seq", axis=1, tiled=True),
    )
    key_blocks = split_blocks(key_all, block)
    value_blocks = split_blocks(value_all, block)

    def visit_back(query_sum, item):
        number, key_block, value_block = item
        key_pos = number * block + row_steps

        def live(carried):
            probs_low, score_grad = score_parts(
                query_rot,
                query_pos,
                attended_heads_grad,
                logsum,
                delta,
                key_block,
                value_block,
                key_pos,
                scale,
            )
            carried = (
                carried
                + jnp.einsum(
                    "shqk,skhe->sqhe", score_grad, key_block, preferred_element_type=jnp.float32
                )
                * scale
            )
            key_term = (
                jnp.einsum(
                    "shqk,sqhe->skhe", score_grad, query_rot, preferred_element_type=jnp.float32
                )
                * scale
            )
            value_term = jnp.einsum(
                "shqk,sqhe->skhe",
                probs_low,
                attended_heads_grad,
                preferred_element_type=jnp.float32,
            )
            joined = jnp.concatenate(
                [key_term.reshape(seqs, block, width), value_term.reshape(seqs, block, width)],
                axis=2,
            )
            return (carried, jnp.swapaxes(joined, 0, 1))

        def empty(carried):
            return (carried, jnp.zeros((block, seqs, 2 * width), jnp.float32))

        return lax.cond(number <= seq_place, live, empty, query_sum)

    query_grad_sum, grad_terms = lax.scan(
        visit_back, zero_heads, (jnp.arange(seq_count, dtype=jnp.int32), key_blocks, value_blocks)
    )
    grad_terms = grad_terms.reshape(seq_count * block, seqs, 2 * width)
    key_value_sum = jnp.swapaxes(
        lax.psum_scatter(
            grad_terms.astype(jnp.bfloat16), "seq", scatter_dimension=0, tiled=True
        ).astype(jnp.float32),
        0,
        1,
    )
    key_grad_sum = key_value_sum[..., :width].reshape(seqs, block, HEADS, head_dim)
    value_grad_sum = key_value_sum[..., width:]
    query_grad = rotate(rounded(query_grad_sum), cosine, -sine)
    key_grad = rotate(rounded(key_grad_sum), cosine, -sine)
    mixed_grad = jnp.concatenate(
        [
            query_grad.reshape(rows, width),
            key_grad.reshape(rows, width),
            value_grad_sum.reshape(rows, width),
        ],
        axis=1,
    ).astype(jnp.bfloat16)
    in_weight_grad = jnp.dot(normed_attn.T, mixed_grad, preferred_element_type=jnp.float32)
    in_bias_grad = jnp.sum(mixed_grad.astype(jnp.float32), axis=0)
    normed_attn_grad = jnp.dot(
        mixed_grad, backward_weights[0].T, preferred_element_type=jnp.float32
    )
    _, attn_pull = jax.vjp(layer_norm, floats, attn_gain, attn_shift)
    attn_token_grad, attn_gain_grad, attn_shift_grad = attn_pull(normed_attn_grad)
    _, ff_pull = jax.vjp(layer_norm, floats, ff_gain, ff_shift)
    ff_token_grad, ff_gain_grad, ff_shift_grad = ff_pull(normed_ff_grad)
    token_grad = (
        (grad_out + attn_token_grad + ff_token_grad)
        .astype(jnp.bfloat16)
        .reshape(seqs, block, width)
    )
    summed = (
        lax.psum_scatter(in_weight_grad, ("dp", "seq"), scatter_dimension=0, tiled=True),
        lax.psum_scatter(in_bias_grad[: 2 * width], ("dp", "seq"), scatter_dimension=0, tiled=True),
        lax.psum_scatter(in_bias_grad[2 * width :], ("dp", "seq"), scatter_dimension=0, tiled=True),
        lax.psum_scatter(out_weight_grad, ("dp", "seq"), scatter_dimension=0, tiled=True),
        lax.psum_scatter(out_bias_grad, ("dp", "seq"), scatter_dimension=0, tiled=True),
        lax.psum_scatter(up_weight_grad, ("dp", "seq"), scatter_dimension=0, tiled=True),
        lax.psum_scatter(up_bias_grad, ("dp", "seq"), scatter_dimension=0, tiled=True),
        lax.psum_scatter(down_weight_grad, ("dp", "seq"), scatter_dimension=0, tiled=True),
        lax.psum_scatter(out_bias_grad, ("dp", "seq"), scatter_dimension=0, tiled=True),
        lax.psum_scatter(attn_gain_grad, ("dp", "seq"), scatter_dimension=0, tiled=True),
        lax.psum_scatter(attn_shift_grad, ("dp", "seq"), scatter_dimension=0, tiled=True),
        lax.psum_scatter(ff_gain_grad, ("dp", "seq"), scatter_dimension=0, tiled=True),
        lax.psum_scatter(ff_shift_grad, ("dp", "seq"), scatter_dimension=0, tiled=True),
    )
    return (
        output,
        token_grad,
        summed[0],
        summed[1],
        summed[2],
        summed[3],
        summed[4],
        summed[5],
        summed[6],
        summed[7],
        summed[8],
        summed[9],
        summed[10],
        summed[11],
        summed[12],
    )


def solution(mesh):
    placed = (
        P("dp", "seq", None),
        P(("dp", "seq"), None),
        P(("dp", "seq")),
        P(("dp", "seq"), None),
        P(("dp", "seq")),
        P(("dp", "seq"), None),
        P(("dp", "seq")),
        P(("dp", "seq"), None),
        P(("dp", "seq")),
        P(("dp", "seq")),
        P(("dp", "seq")),
        P(("dp", "seq")),
        P(("dp", "seq")),
        P("dp", "seq", None),
    )
    return jax.shard_map(
        on_device,
        mesh=mesh,
        in_specs=placed,
        out_specs=(
            P("dp", "seq", None),
            P("dp", "seq", None),
            P(("dp", "seq"), None),
            P(("dp", "seq")),
            P(("dp", "seq")),
            P(("dp", "seq"), None),
            P(("dp", "seq")),
            P(("dp", "seq"), None),
            P(("dp", "seq")),
            P(("dp", "seq"), None),
            P(("dp", "seq")),
            P(("dp", "seq")),
            P(("dp", "seq")),
            P(("dp", "seq")),
            P(("dp", "seq")),
        ),
        check_vma=False,
    )
```

profile of v0, /device:TPU:0, one launch (start us, length us, event | category | flops | bytes accessed | tf_op | source)
XLA Modules:
  0.0 1661.4 jit_solution(1948110149167394661)
XLA Ops:
  14.6 42.9 %all-reduce.16 = (bf16[1024]{0:T(1024)(128)(2,1)}, bf16[1024]{0:T(1024)(128)(2,1)}, bf16[3072]{0:T(1024)(128)(2,1)S(1)}, bf16[1024]{0:T(1024)(128)(2,1)S(1)}, bf...) all-reduce(bf16[1024]{0:T(1024)(128)(2,1)S(1)} %dynamic-update-slic, ...), channel_id=1, replica_groups=mesh['dp'=8,'seq'=4] {'dp','seq'}, use_global_device_ids=true, to_apply=%add.5 | all-reduce | flops 9216 | bytes 36864
  61.8 21.5 %all-gather.9.cloned.1.call-done = bf16[1024,3072]{1,0:T(8,128)(2,1)} async-done(((bf16[32,3072]{1,0:T(8,128)(2,1)}), bf16[1024,3072]{1,0:T(8,128)(2,1)}) %all-gather.9.cloned.1.call-update) | async-done | bytes 6291472 | tf_op jit(solution)/shard_map/all_gather | solution.py:108
  83.3 6.1 convolution_add_fusion
  93.9 2.9 copy.65
  104.2 2.7 slice.158
  108.4 32.7 %all-gather.13.cloned.1.call-done = bf16[1024,1024]{1,0:T(8,128)(2,1)} async-done(((bf16[32,1024]{1,0:T(8,128)(2,1)}), bf16[1024,1024]{1,0:T(8,128)(2,1)}) %all-gather.13.cloned.1.call-update) | async-done | bytes 2097168 | tf_op jit(solution)/shard_map/all_gather | solution.py:110
  141.1 2.9 convolution_convert_fusion
  146.9 48.0 %all-gather.11.cloned.1.call-done = bf16[1,2048,1024]{1,2,0:T(8,128)(2,1)} async-done(((bf16[1,512,1024]{1,2,0:T(8,128)(2,1)}), bf16[1,2048,1024]{1,2,0:T(8,128)(2,1)}) %all-gather.11.cloned.1.call-update) | async-done | bytes 4194320 | tf_op jit(solution)/shard_map/all_gather | solution.py:156
  195.0 7.8 transpose_reshape.8
  202.8 5.6 copy.68
  208.4 41.0 %all-gather.19.cloned.1.call-done = bf16[2048,1024]{1,0:T(8,128)(2,1)} async-done(((bf16[512,1024]{1,0:T(8,128)(2,1)}), bf16[2048,1024]{1,0:T(8,128)(2,1)}) %all-gather.19.cloned.1.call-update) | async-done | bytes 4194320 | tf_op jit(solution)/shard_map/all_gather | solution.py:157
  249.4 11.6 reshape.630
  261.0 9.8 copy.69
  271.1 19.3 %while.33 = (s32[]{:T(128)}, f32[1,16,512]{2,1,0:T(8,128)S(1)}, f32[1,16,512]{2,1,0:T(8,128)S(1)}, f32[1,512,16,64]{1,3,2,0:T(8,128)S(1)}, s32[4]{0:T(128)S(1)},...) while((s32[]{:T(128)}, f32[1,16,512]{2,1,0:T(8,128)S(1)}, ...), condition=%wide.region_7.8_spmd.clone, body=%wide.region_2.7_spmd.clone.sunk | while | flops 1129604096 | bytes 59260208 | solution.py:170
  272.4 14.2 conditional.6
  272.6 3.9 fusion.8
  276.5 6.0 bitcast_add_fusion
  282.5 4.0 fusion.10
  293.3 81.4 %while.34 = (s32[]{:T(128)}, f32[1,512,16,64]{1,3,2,0:T(8,128)S(1)}, bf16[4,512,1,2048]{3,1,0,2:T(8,128)(2,1)}, s32[4]{0:T(128)S(1)}, s32[]{:T(128)}, /*index=5*...) while((s32[]{:T(128)}, ...), condition=%wide.region_12.13_spmd.clone, body=%wide.region_9.12_spmd.clone.sunk | while | flops 2732852224 | bytes 136167728 | solution.py:273
  295.0 43.0 %conditional.7 = (f32[1,512,16,64]{1,3,2,0:T(8,128)S(1)}, bf16[1,512,1,2048]{1,3,2,0:T(8,128)(2,1)}) conditional(s32[]{:T(128)} %convert_element_type.313, f32[1,512,16,64]{1,3,2,0:T(8,128)S(1)} %get-tuple-element.849, (bf16[4,1,512,16,64]{2,4,3,1,0:T(8,128)(2,1)}, s32[]{:T(128)}, s32[]{:T(128)}, s32[512]{0:T(512)S(1)}, s32[]{:T(128)}, ...), branch_computations={%region_10.10_spmd, %region_11.11_spmd} | conditional | flops 2732852224 | bytes 127776320 | solution.py:271
  295.0 10.3 fusion.37
  306.2 9.5 fusion.28
  315.7 3.6 convolution_multiply_fusion
  319.3 10.5 fusion.30
  329.8 3.0 maximum_bitcast_fusion
  332.8 5.1 bitcast_add_fusion.2
  338.0 4.0 copy.100
  342.0 3.1 constant_dynamic-update-slice_fusion.2
  347.8 4.0 copy.100
  351.8 3.2 constant_dynamic-update-slice_fusion.2
  357.7 4.0 copy.100
  361.6 3.1 constant_dynamic-update-slice_fusion.2
  367.5 4.0 copy.100
  371.5 3.2 constant_dynamic-update-slice_fusion.2
  375.4 229.2 %all-gather.1 = bf16[32,1,128]{2,1,0:T(2,128)(2,1)S(1)} all-gather(bf16[1,1,128]{2,1,0:T(2,128)(2,1)S(1)} %bitcast.251), channel_id=1, replica_groups=mesh['dp'=8,'seq'=4] {'dp','seq'}, dimensions={0}, use_global_device_ids=true | all-gather | bytes 8448 | tf_op jit(solution)/shard_map/all_gather | solution.py:113
  604.6 4.5 fusion.84
  610.4 27.6 %multiply_convert_fusion = (bf16[512,4096]{1,0:T(8,128)(2,1)}, f32[512,4096]{1,0:T(8,128)}, f32[512,4096]{1,0:T(8,128)}) fusion(f32[4096]{0:T(1024)S(1)} %bitcast.249, bf16[1024,4096]{1,0:T(8,128)(2,1)} %all-gather.15.cloned.1.call-done, bf16[1,512,1024]{2,1,0:T(8,128)(2,1)S(1)} %copy-done.1, f32[1024]{0:T(1024)S(1)} %convert_element_type.183, ...), kind=kOutput, calls=%fused_computation.63 | convolution fusion | flops 4436525056 | bytes 30437376 | tf_op jit(solution)/shard_map/dot_general | solution.py:181
  637.9 13.6 convert_reduce_fusion
  653.6 8.4 fusion.104
  662.3 12.8 fusion.82
  689.0 9.4 fusion.108
  699.1 8.4 fusion.120
  707.5 7.1 fusion.119
  718.0 4.0 fusion.115
  726.6 38.3 %all-reduce.15 = (f32[2048]{0:T(1024)S(1)}, f32[1024]{0:T(1024)S(1)}, f32[1024]{0:T(1024)S(1)}, f32[4096]{0:T(1024)S(1)}, f32[1024]{0:T(1024)S(1)}, /*index=5*/f...) all-reduce(f32[2048]{0:T(1024)S(1)} %slice-done.1, ...), channel_id=5, replica_groups=mesh['dp'=8,'seq'=4] {'dp','seq'}, use_global_device_ids=true, to_apply=%region_20.21.clone | all-reduce | flops 12288 | bytes 98304
  769.1 358.1 %reduce-scatter.12.cloned.1.call-done = f32[32,4096]{1,0:T(8,128)} async-done(((f32[1024,4096]{1,0:T(8,128)}), f32[32,4096]{1,0:T(8,128)}) %reduce-scatter.12.cloned.1.call-update) | async-done | bytes 524304 | tf_op jit(solution)/shard_map/reduce_scatter | solution.py:316
  1127.2 361.9 %reduce-scatter.14.cloned.1.call-done = f32[128,1024]{1,0:T(8,128)} async-done(((f32[4096,1024]{1,0:T(8,128)}), f32[128,1024]{1,0:T(8,128)}) %reduce-scatter.14.cloned.1.call-update) | async-done | bytes 524304 | tf_op jit(solution)/shard_map/reduce_scatter | solution.py:318
  1489.1 164.8 %reduce-scatter.8.cloned.1.call-done = f32[32,3072]{1,0:T(8,128)} async-done(((f32[1024,3072]{1,0:T(8,128)}), f32[32,3072]{1,0:T(8,128)}) %reduce-scatter.8.cloned.1.call-update) | async-done | bytes 393232 | tf_op jit(solution)/shard_map/reduce_scatter | solution.py:311
  (218 shorter events, 75.9 us)
Async XLA Ops:
  7.2 76.1 %all-gather.9.cloned.1.call-start = ((), (), s32[]{:S(2)}) async-start(), calls=%async_computation.5 | async-start | bytes 6488064 | tf_op jit(solution)/shard_map/all_gather | solution.py:108
  7.9 133.2 %all-gather.13.cloned.1.call-start = ((), (), s32[]{:S(2)}) async-start(), calls=%async_computation.7 | async-start | bytes 2162688 | tf_op jit(solution)/shard_map/all_gather | solution.py:110
  8.7 186.3 %all-gather.11.cloned.1.call-start = ((), (), s32[]{:S(2)}) async-start(), calls=%async_computation.6 | async-start | bytes 5242880 | tf_op jit(solution)/shard_map/all_gather | solution.py:156
  57.5 25.8 %copy-start.12 = (f32[1024]{0:T(1024)}, f32[1024]{0:T(1024)S(1)}, u32[]{:S(2)}) copy-start(f32[1024]{0:T(1024)S(1)} %convert_element_type.173) | copy-start | bytes 12292
  57.5 25.8 %copy-start.14 = (f32[1024]{0:T(1024)}, f32[1024]{0:T(1024)S(1)}, u32[]{:S(2)}) copy-start(f32[1024]{0:T(1024)S(1)} %convert_element_type.174) | copy-start | bytes 12292
  58.3 43.2 %copy-start.16 = (f32[512,16]{0,1:T(8,128)}, f32[512,16]{0,1:T(8,128)S(1)}, u32[]{:S(2)}) copy-start(f32[512,16]{0,1:T(8,128)S(1)} %get-tuple-element.636) | copy-start | bytes 98308
  60.1 23.2 %copy-start.18 = (f32[512]{0:T(512)}, f32[512]{0:T(512)S(1)}, u32[]{:S(2)}) copy-start(f32[512]{0:T(512)S(1)} %broadcast_multiply_fusion.1) | copy-start | bytes 6148
  61.7 21.6 %copy-start.24 = (f32[512]{0:T(512)}, f32[512]{0:T(512)S(1)}, u32[]{:S(2)}) copy-start(f32[512]{0:T(512)S(1)} %fusion.73) | copy-start | bytes 6148
  61.8 21.6 %copy-start.20 = (f32[512]{0:T(512)}, f32[512]{0:T(512)S(1)}, u32[]{:S(2)}) copy-start(f32[512]{0:T(512)S(1)} %fusion.102) | copy-start | bytes 6148
  89.4 2.6 copy-start.4
  101.5 39.6 %copy-start.6 = (bf16[1,512,1024]{2,1,0:T(8,128)(2,1)S(1)}, bf16[1,512,1024]{2,1,0:T(8,128)(2,1)}, u32[]{:S(2)}) copy-start(bf16[1,512,1024]{2,1,0:T(8,128)(2,1)} %param.35) | copy-start | bytes 3145732
  104.2 145.2 %all-gather.19.cloned.1.call-start = ((), (), s32[]{:S(2)}) async-start(), calls=%async_computation.15 | async-start | bytes 5242880 | tf_op jit(solution)/shard_map/all_gather | solution.py:157
  107.0 502.4 %all-gather.15.cloned.1.call-start = ((), (), s32[]{:S(2)}) async-start(), calls=%async_computation.8 | async-start | bytes 8650752 | tf_op jit(solution)/shard_map/all_gather | solution.py:112
  107.6 530.4 %all-gather.17.cloned.1.call-start = ((), (), s32[]{:S(2)}) async-start(), calls=%async_computation.9 | async-start | bytes 8650752 | tf_op jit(solution)/shard_map/all_gather | solution.py:114
  108.1 569.6 %reduce-scatter.6.cloned.1.call-start = ((), (), s32[]{:S(2)}) async-start(), calls=%async_computation.10 | async-start | bytes 10485760 | tf_op jit(solution)/shard_map/reduce_scatter | solution.py:278
  315.7 3.6 copy-start
  374.7 0.7 copy-start.28
  374.7 0.7 copy-start.30
  374.7 229.9 %copy-start.7 = (bf16[1,512,1024]{2,1,0:T(8,128)(2,1)S(1)}, bf16[1,512,1024]{2,1,0:T(8,128)(2,1)}, u32[]{:S(2)}) copy-start(bf16[1,512,1024]{2,1,0:T(8,128)(2,1)} %param.35) | copy-start | bytes 3145732
  374.7 394.4 %reduce-scatter.10.cloned.1.call-start = ((), (), s32[]{:S(2)}) async-start(), calls=%async_computation.12 | async-start | bytes 4325376 | tf_op jit(solution)/shard_map/reduce_scatter | solution.py:314
  609.1 1.2 copy-start.1
  609.1 1.2 copy-start.19
  609.1 1.2 copy-start.21
  609.1 518.0 %reduce-scatter.12.cloned.1.call-start = ((), (), s32[]{:S(2)}) async-start(), calls=%async_computation.13 | async-start | bytes 17301504 | tf_op jit(solution)/shard_map/reduce_scatter | solution.py:316
  651.5 2.1 copy-start.34
  662.0 827.0 %reduce-scatter.14.cloned.1.call-start = ((), (), s32[]{:S(2)}) async-start(), calls=%async_computation.14 | async-start | bytes 17301504 | tf_op jit(solution)/shard_map/reduce_scatter | solution.py:318
  675.1 978.7 %reduce-scatter.8.cloned.1.call-start = ((), (), s32[]{:S(2)}) async-start(), calls=%async_computation.11 | async-start | bytes 12976128 | tf_op jit(solution)/shard_map/reduce_scatter | solution.py:311
  675.3 1.0 copy-start.2
  675.6 1.4 copy-start.5
  680.4 1.9 copy-start.17
  680.4 1.9 copy-start.22
  681.0 1.3 copy-start.10
  681.0 3.4 slice-start
  684.3 1.0 copy-start.11
  684.3 4.6 copy-start.13
  684.3 4.7 copy-start.15
  699.1 8.4 copy-start.33
  699.1 18.9 %slice-start.3 = ((s8[6291456]{0:T(1024)(128)(4,1)}), s8[4194304]{0:T(1024)(128)(4,1)S(1)}, s32[]{:S(2)}) async-start(s8[6291456]{0:T(1024)(128)(4,1)} %bitcast.252), calls=%async_computation.19 | async-start | bytes 8388608
  707.5 7.2 copy-start.9
  707.5 7.2 copy-start.31
  707.5 10.4 slice-start.4
  714.7 2.5 copy-start.3
  717.9 4.0 copy-start.23
  718.0 4.0 copy-start.25
  722.0 2.0 copy-start.8
  724.0 2.6 slice-start.1
  724.0 2.5 slice-start.2
  765.0 889.4 %copy-start.32 = (f32[32]{0:T(128)}, f32[32]{0:T(128)S(1)}, u32[]{:S(2)}) copy-start(f32[32]{0:T(128)S(1)} %dynamic-slice.2) | copy-start | bytes 388
  (3 other events, 2.0 us)
Sparse Core Ops, SparseCore 0:
  10.9 72.3 all-gather.8
  86.2 54.8 all-gather.12
  143.5 51.4 all-gather.10
  196.7 52.6 all-gather.18
  252.1 77.5 all-gather.14
  332.5 76.2 all-gather.16
  411.8 212.3 reduce-scatter.5
  627.1 141.2 reduce-scatter.9
  771.4 355.7 reduce-scatter.11
  1130.0 359.0 reduce-scatter.13
  1496.7 157.1 reduce-scatter.7
where the time goes:
time: 1670 us; the launch traced here: 1660 us
  waiting for transfers between devices  1030 us (62%)
  blocking collectives  310 us (19%)
  matrix products  156 us (9%)
  local copies, waits for them, and re-layouts  112 us (7%)
  other arithmetic  29.3 us (2%)
    reduce_scatter x1, waiting for transfers between devices, on_device(): lax.psum_scatter(down_weight_grad, ('dp', 'seq'), scatter_dimension=0, ti...  362 us
    reduce_scatter x1, waiting for transfers between devices, on_device(): lax.psum_scatter(up_weight_grad, ('dp', 'seq'), scatter_dimension=0, tile...  358 us
    all_gather x1, blocking collectives, on_device(): lax.all_gather(up_bias, ('dp', 'seq'), axis=0, tiled=True)  229 us
    reduce_scatter x1, waiting for transfers between devices, on_device(): lax.psum_scatter(in_weight_grad, ('dp', 'seq'), scatter_dimension=0, tile...  165 us
    unnamed x2, blocking collectives  81.3 us
    all_gather x1, waiting for transfers between devices, on_device(): lax.all_gather(key_flat, 'seq', axis=1, tiled=True)  48 us
    all_gather x1, waiting for transfers between devices, on_device(): lax.all_gather(value_part, 'seq', axis=1, tiled=True)  41 us
    unnamed x97, local copies, waits for them, and re-layouts  34.7 us
  transfers between devices with their start and end apart: 11, of which 7 were waited for; matrix products, arithmetic and copies ran while one was open for 17% of the time, Pallas kernels for 0%

commit v1 on v0

v1 whole, which is shorter than its diff:
```python
import functools
import math

import jax
import jax.numpy as jnp
import numpy as np
from jax import lax
from jax.experimental import pallas as pl
from jax.experimental.pallas import tpu as pltpu
from jax.sharding import PartitionSpec as P

HEADS = 16
ROT = 16

norm_eps = 1e-05
masked_score = -1e30
low = jnp.bfloat16
full = jnp.float32
kernel_memory = 56 * 1024 * 1024


def place_at(pieces, spots, axis):
    count = len(pieces)
    shape = list(pieces[0].shape)
    shape.insert(axis, count)
    held = jnp.zeros(shape, pieces[0].dtype)
    for piece, spot in zip(pieces, spots):
        held = lax.dynamic_update_index_in_dim(held, piece, spot, axis)
    return held


def pick(array, spot, axis):
    return lax.dynamic_index_in_dim(array, spot, axis, keepdims=False)


class Layout:
    def __init__(self):
        self.dp = lax.axis_size("dp")
        self.seq = lax.axis_size("seq")
        self.cores = 2 if self.dp % 2 == 0 else 1
        self.line = self.dp // self.cores
        place = lax.axis_index("dp")
        self.core = place % self.cores
        self.z = place // self.cores
        self.rank = lax.axis_index("seq")

    def seq_swap(self, array, k):
        return lax.ppermute(array, "seq", [(i, i ^ k) for i in range(self.seq)])

    def core_swap(self, array):
        return lax.ppermute(array, "dp", [(i, i ^ 1) for i in range(self.dp)])

    def z_shift(self, array, k):
        c = self.cores
        pairs = [(i, i + k * c) for i in range(self.dp) if 0 <= i + k * c < self.dp]
        return lax.ppermute(array, "dp", pairs)

    def z_turn(self, array, k):
        c = self.cores
        return lax.ppermute(array, "dp", [(i, (i + k * c) % self.dp) for i in range(self.dp)])

    def seq_exchange(self, piece_for):
        return [piece_for(self.rank)] + [
            self.seq_swap(piece_for(self.rank ^ k), k) for k in range(1, self.seq)
        ]

    def seq_spots(self):
        return [self.rank ^ k for k in range(self.seq)]

    def seq_gather(self, array):
        if self.seq != 4:
            return [array] + [self.seq_swap(array, k) for k in range(1, self.seq)]
        half = array.shape[1] // 2
        first, second = array[:, :half], array[:, half:]
        x_first = self.seq_swap(first, 1)
        y_second = self.seq_swap(second, 2)
        x_second = self.seq_swap(second, 1)
        y_first = self.seq_swap(first, 2)
        d_first = self.seq_swap(x_first, 2)
        d_second = self.seq_swap(y_second, 1)
        return [
            array,
            jnp.concatenate([x_first, x_second], 1),
            jnp.concatenate([y_first, y_second], 1),
            jnp.concatenate([d_first, d_second], 1),
        ]

    def seq_reduce(self, parts):
        if self.seq != 4:
            total = parts[0].astype(full)
            for k in range(1, self.seq):
                total = total + self.seq_swap(parts[k].astype(low), k).astype(full)
            return total
        half = parts[0].shape[1] // 2
        p1, p2, p3 = parts[1].astype(low), parts[2].astype(low), parts[3].astype(low)
        for_y = self.seq_swap(p3[:, :half], 1)
        for_x = self.seq_swap(p3[:, half:], 2)
        r1_first = self.seq_swap(p1[:, :half], 1)
        r2_second = self.seq_swap(p2[:, half:], 2)
        r1_second = self.seq_swap(
            (p1[:, half:].astype(full) + for_x.astype(full)).astype(low), 1
        )
        r2_first = self.seq_swap(
            (p2[:, :half].astype(full) + for_y.astype(full)).astype(low), 2
        )
        first = r1_first.astype(full) + r2_first.astype(full)
        second = r1_second.astype(full) + r2_second.astype(full)
        return parts[0].astype(full) + jnp.concatenate([first, second], 1)

    def dp_gather(self, array):
        right = left = array
        rights, lefts = [], []
        for _ in range(self.line - 1):
            right = self.z_shift(right, 1)
            left = self.z_shift(left, -1)
            rights.append(right)
            lefts.append(left)
        row = jnp.stack(rights[::-1] + [array] + lefts, 0)
        mine = lax.dynamic_slice_in_dim(row, self.line - 1 - self.z, self.line, 0)
        if self.cores == 1:
            return mine
        other = self.core_swap(mine)
        both = lax.dynamic_slice_in_dim(jnp.stack([mine, other, mine], 1), self.core, 2, 1)
        return both.reshape((self.dp,) + array.shape)

    def dp_reduce(self, array):
        if self.cores == 2:
            pairs = array.reshape((self.line, 2) + array.shape[1:])
            other = self.core_swap(pick(pairs, 1 - self.core, 1).astype(low))
            array = pick(pairs, self.core, 1).astype(full) + other.astype(full)

        def chunk(spot):
            return pick(array, jnp.clip(spot, 0, self.line - 1), 0)

        right = chunk(self.z + self.line - 1)
        left = chunk(self.z - self.line + 1)
        for step in range(1, self.line):
            far = self.line - 1 - step
            right = self.z_shift(right.astype(low), 1).astype(full)
            left = self.z_shift(left.astype(low), -1).astype(full)
            if far > 0:
                right = right + chunk(self.z + far)
                left = left + chunk(self.z - far)
        return chunk(self.z) + right + left

    def small_gather(self, vector):
        pieces = [vector] + [self.seq_swap(vector, k) for k in range(1, self.seq)]
        held = place_at(pieces, self.seq_spots(), 0)
        if self.cores == 2:
            held = place_at([held, self.core_swap(held)], [self.core, 1 - self.core], 0)
        else:
            held = held[None]
        pieces = [held] + [self.z_turn(held, k) for k in range(1, self.line)]
        spots = [(self.z - k) % self.line for k in range(self.line)]
        held = place_at(pieces, spots, 0)
        return held.reshape((self.dp, self.seq) + vector.shape)

    def small_reduce(self, array):
        array = sum(self.seq_exchange(lambda spot: pick(array, spot, 1)))
        if self.cores == 2:
            pairs = array.reshape((self.line, 2) + array.shape[1:])
            array = pick(pairs, self.core, 1) + self.core_swap(pick(pairs, 1 - self.core, 1))
        total = pick(array, self.z, 0)
        for k in range(1, self.line):
            total = total + self.z_turn(pick(array, (self.z + k) % self.line, 0), k)
        return total


def rotary_tables(length, lanes, head_dim):
    half = ROT // 2
    exponent = -np.arange(0, ROT, 2, dtype=np.float32) / np.float32(ROT)
    frequency = np.float32(10000.0) ** exponent
    phase = np.arange(length, dtype=np.float32)[:, None] * frequency[None, :]
    cosine = np.ones((length, head_dim), np.float32)
    sine = np.zeros((length, head_dim), np.float32)
    cosine[:, :half] = cosine[:, half:ROT] = np.cos(phase)
    sine[:, :half] = -np.sin(phase)
    sine[:, half:ROT] = np.sin(phase)
    copies = lanes // head_dim
    return np.tile(cosine, (1, copies)), np.tile(sine, (1, copies))


def roll_lanes(x, shift):
    size = x.shape[-1]
    if size % 128 == 0:
        return pltpu.roll(x, shift % size, x.ndim - 1)
    return jnp.roll(x, shift, -1)


def turn(x, cosine, sine, head_dim):
    half = ROT // 2
    lane = lax.broadcasted_iota(jnp.int32, x.shape, 1) % head_dim
    swapped = jnp.where(lane < half, roll_lanes(x, -half), roll_lanes(x, half))
    return x * cosine + swapped * sine


def normalised(x):
    mean = jnp.mean(x, axis=-1, keepdims=True)
    centered = x - mean
    variance = jnp.mean(centered * centered, axis=-1, keepdims=True)
    rstd = lax.rsqrt(variance + norm_eps)
    return centered * rstd, rstd


def project_kernel(head_dim, lanes, place, x_ref, weight_ref, bias_ref, norms_ref, cos_ref, sin_ref, attn_ref, ff_ref, qkv_ref):
    unit, _ = normalised(x_ref[...].astype(full))
    normed = (unit * norms_ref[0:1, :] + norms_ref[1:2, :]).astype(low)
    attn_ref[...] = normed
    ff_ref[...] = (unit * norms_ref[2:3, :] + norms_ref[3:4, :]).astype(low)
    mixed = jnp.dot(normed, weight_ref[...], preferred_element_type=full) + bias_ref[...]
    cosine, sine = cos_ref[...], sin_ref[...]
    for group in range(mixed.shape[1] // lanes):
        span = slice(group * lanes, (group + 1) * lanes)
        part = mixed[:, span]
        if group % 3 < 2:
            part = turn(part, cosine, sine, head_dim)
        qkv_ref[:, span] = part.astype(low)


def project(place, x, weight, bias, norms, cosine, sine, block, seqs, lanes, head_dim):
    rows, width = x.shape
    columns = weight.shape[1]
    whole = lambda i, place: (0, 0)
    step = lambda i, place: (i, 0)
    spot = lambda i, place: ((i // seqs) ^ place[0], 0)
    return pl.pallas_call(
        functools.partial(project_kernel, head_dim, lanes),
        grid_spec=pltpu.PrefetchScalarGridSpec(
            num_scalar_prefetch=1,
            grid=(rows // block,),
            in_specs=[
                pl.BlockSpec((block, width), step),
                pl.BlockSpec((width, columns), whole),
                pl.BlockSpec((1, columns), whole),
                pl.BlockSpec((4, width), whole),
                pl.BlockSpec((block, lanes), spot),
                pl.BlockSpec((block, lanes), spot),
            ],
            out_specs=[
                pl.BlockSpec((block, width), step),
                pl.BlockSpec((block, width), step),
                pl.BlockSpec((block, columns), step),
            ],
        ),
        out_shape=[
            jax.ShapeDtypeStruct((rows, width), low),
            jax.ShapeDtypeStruct((rows, width), low),
            jax.ShapeDtypeStruct((rows, columns), low),
        ],
        compiler_params=pltpu.CompilerParams(vmem_limit_bytes=kernel_memory),
        name="project",
    )(place, x, weight, bias, norms, cosine, sine)


def contract(a, b, da, db):
    return lax.dot_general(a, b, (((da,), (db,)), ((), ())), preferred_element_type=full)


def head_lanes(x, head, pair, head_dim):
    if pair == 1:
        return x
    lane = lax.broadcasted_iota(jnp.int32, x.shape, 1)
    inside = (lane >= head * head_dim) & (lane < (head + 1) * head_dim)
    return jnp.where(inside, x, jnp.zeros_like(x))


def attend_kernel(pair, head_dim, place, qkv_ref, exact_ref, low_ref, lse_ref):
    count, block, lanes3 = qkv_ref.shape
    lanes = lanes3 // 3
    scale = 1.0 / math.sqrt(head_dim)
    s = place[0]
    row = lax.broadcasted_iota(jnp.int32, (block, block), 0)
    column = lax.broadcasted_iota(jnp.int32, (block, block), 1)
    for i in range(count):
        here = i ^ s
        query = qkv_ref[here, :, 0:lanes] * jnp.asarray(scale, low)
        joined = jnp.zeros((block, lanes), full)
        for head in range(pair):
            mine = head_lanes(query, head, pair, head_dim)
            scores = []
            for j in range(i + 1):
                part = contract(mine, qkv_ref[j ^ s, :, lanes : 2 * lanes], 1, 1)
                if j == i:
                    part = jnp.where(column <= row, part, masked_score)
                scores.append(part)
            top = functools.reduce(jnp.maximum, scores)
            top = jnp.max(top, axis=-1, keepdims=True)
            total = None
            update = None
            for j in range(i + 1):
                weights = jnp.exp(scores[j] - top)
                term = jnp.dot(
                    weights.astype(low), qkv_ref[j ^ s, :, 2 * lanes :], preferred_element_type=full
                )
                update = term if update is None else update + term
                total = weights if total is None else total + weights
            total = jnp.sum(total, axis=-1, keepdims=True)
            joined = joined + head_lanes(update / total, head, pair, head_dim)
            lse = jnp.broadcast_to(top + jnp.log(total), (block, 128))
            lse_ref[here, head : head + 1, :] = jnp.transpose(lse)[0:1, :]
        exact_ref[here] = joined
        low_ref[here] = joined.astype(low)


def attend(place, qkv, pair, head_dim):
    count, seqs, block, columns = qkv.shape
    lanes = pair * head_dim
    groups = columns // (3 * lanes)
    spec = lambda width: pl.BlockSpec((count, None, block, width), lambda b, g, place: (0, b, 0, g))
    return pl.pallas_call(
        functools.partial(attend_kernel, pair, head_dim),
        grid_spec=pltpu.PrefetchScalarGridSpec(
            num_scalar_prefetch=1,
            grid=(seqs, groups),
            in_specs=[spec(3 * lanes)],
            out_specs=[
                spec(lanes),
                spec(lanes),
                pl.BlockSpec((count, None, None, pair, block), lambda b, g, place: (0, b, g, 0, 0)),
            ],
        ),
        out_shape=[
            jax.ShapeDtypeStruct((count, seqs, block, groups * lanes), full),
            jax.ShapeDtypeStruct((count, seqs, block, groups * lanes), low),
            jax.ShapeDtypeStruct((count, seqs, groups, pair, block), full),
        ],
        compiler_params=pltpu.CompilerParams(vmem_limit_bytes=kernel_memory),
        name="attend",
    )(place, qkv)


def attend_back_kernel(pair, head_dim, place, qkv_ref, exact_ref, grad_ref, lse_ref, cos_ref, sin_ref, out_ref, key_ref, value_ref):
    count, block, lanes3 = qkv_ref.shape
    lanes = lanes3 // 3
    scale = 1.0 / math.sqrt(head_dim)
    s = place[0]
    row = lax.broadcasted_iota(jnp.int32, (block, block), 0)
    column = lax.broadcasted_iota(jnp.int32, (block, block), 1)
    key_ref[...] = jnp.zeros_like(key_ref)
    value_ref[...] = jnp.zeros_like(value_ref)

    def back(total, at):
        kept = total.astype(low).astype(full)
        return turn(kept, cos_ref[at], -sin_ref[at], head_dim).astype(low)

    for i in range(count):
        here = i ^ s
        query = qkv_ref[here, :, 0:lanes] * jnp.asarray(scale, low)
        grad = grad_ref[here]
        product = exact_ref[here] * grad.astype(full)
        joined = jnp.zeros((block, lanes), full)
        for head in range(pair):
            mine = head_lanes(query, head, pair, head_dim)
            mine_grad = head_lanes(grad, head, pair, head_dim)
            delta = jnp.sum(
                jnp.transpose(head_lanes(product, head, pair, head_dim)), axis=0, keepdims=True
            )
            lse = lse_ref[here, head : head + 1, :]
            update = None
            for j in range(i + 1):
                there = j ^ s
                key = qkv_ref[there, :, lanes : 2 * lanes]
                value = qkv_ref[there, :, 2 * lanes :]
                scores = contract(key, mine, 1, 1)
                if j == i:
                    scores = jnp.where(row <= column, scores, masked_score)
                probs = jnp.exp(scores - lse)
                prob_grad = contract(value, mine_grad, 1, 1)
                score_grad = (probs * (prob_grad - delta)).astype(low)
                value_ref[j] += jnp.dot(probs.astype(low), mine_grad, preferred_element_type=full)
                key_ref[j] += jnp.dot(score_grad, mine, preferred_element_type=full)
                term = contract(score_grad, key, 0, 0)
                update = term if update is None else update + term
            joined = joined + head_lanes(update, head, pair, head_dim)
        out_ref[here, :, 0:lanes] = back(joined * scale, here)
    for j in range(count):
        there = j ^ s
        out_ref[there, :, lanes : 2 * lanes] = back(key_ref[j], there)
        out_ref[there, :, 2 * lanes :] = value_ref[j].astype(low)


def attend_back(place, qkv, exact, grad, lse, cosine, sine, pair, head_dim):
    count, seqs, block, columns = qkv.shape
    lanes = pair * head_dim
    groups = columns // (3 * lanes)
    spec = lambda width: pl.BlockSpec((count, None, block, width), lambda b, g, place: (0, b, 0, g))
    table = pl.BlockSpec((count, block, lanes), lambda b, g, place: (0, 0, 0))
    return pl.pallas_call(
        functools.partial(attend_back_kernel, pair, head_dim),
        grid_spec=pltpu.PrefetchScalarGridSpec(
            num_scalar_prefetch=1,
            grid=(seqs, groups),
            in_specs=[
                spec(3 * lanes),
                spec(lanes),
                spec(lanes),
                pl.BlockSpec((count, None, None, pair, block), lambda b, g, place: (0, b, g, 0, 0)),
                table,
                table,
            ],
            out_specs=spec(3 * lanes),
            scratch_shapes=[
                pltpu.VMEM((count, block, lanes), full),
                pltpu.VMEM((count, block, lanes), full),
            ],
        ),
        out_shape=jax.ShapeDtypeStruct(qkv.shape, low),
        compiler_params=pltpu.CompilerParams(vmem_limit_bytes=kernel_memory),
        name="attend_back",
    )(place, qkv, exact, grad, lse, cosine, sine)


def unproject_kernel(x_ref, mixed_ref, hidden_ref, in_ref, up_ref, norms_ref, out_ref, sums_ref):
    unit, _ = normalised(x_ref[...].astype(full))
    attn = contract(mixed_ref[...], in_ref[...], 1, 1)
    ff = contract(hidden_ref[...], up_ref[...], 1, 1)
    out_ref[...] = attn * norms_ref[0:1, :] + ff * norms_ref[2:3, :]
    sums = [attn * unit, attn, ff * unit, ff]
    sums = jnp.concatenate([jnp.sum(a, axis=0, keepdims=True) for a in sums], 0)

    @pl.when(pl.program_id(0) == 0)
    def _():
        sums_ref[...] = sums

    @pl.when(pl.program_id(0) > 0)
    def _():
        sums_ref[...] += sums


def unproject(x, mixed, hidden, in_weight, up_weight, norms, block):
    rows, width = x.shape
    whole = lambda i: (0, 0)
    step = lambda i: (i, 0)
    return pl.pallas_call(
        unproject_kernel,
        grid=(rows // block,),
        in_specs=[
            pl.BlockSpec((block, width), step),
            pl.BlockSpec((block, mixed.shape[1]), step),
            pl.BlockSpec((block, hidden.shape[1]), step),
            pl.BlockSpec(in_weight.shape, whole),
            pl.BlockSpec(up_weight.shape, whole),
            pl.BlockSpec((4, width), whole),
        ],
        out_specs=[pl.BlockSpec((block, width), step), pl.BlockSpec((4, width), whole)],
        out_shape=[
            jax.ShapeDtypeStruct((rows, width), full),
            jax.ShapeDtypeStruct((4, width), full),
        ],
        compiler_params=pltpu.CompilerParams(vmem_limit_bytes=kernel_memory),
        name="unproject",
    )(x, mixed, hidden, in_weight, up_weight, norms)


def on_device(
    tokens,
    input_weight,
    input_bias,
    output_weight,
    output_bias,
    up_weight,
    up_bias,
    down_weight,
    down_bias,
    attention_gain,
    attention_shift,
    feedforward_gain,
    feedforward_shift,
    cotangent,
):
    at = Layout()
    dp, seq, rank = at.dp, at.seq, at.rank
    seqs, block, width = tokens.shape
    shard = input_weight.shape[0]
    units = down_weight.shape[0]
    head_dim = width // HEADS
    heads = HEADS // seq
    pair = 2 if heads % 2 == 0 else 1
    groups = heads // pair
    lanes = pair * head_dim
    span = heads * head_dim
    place = rank.astype(jnp.int32).reshape(1)

    vectors = (input_bias, output_bias, up_bias, down_bias, attention_gain, attention_shift, feedforward_gain, feedforward_shift)
    sizes = [v.shape[0] for v in vectors]
    padded = -sum(sizes) % 128
    gathered = at.small_gather(jnp.concatenate(vectors + (jnp.zeros((padded,), low),)))
    edges = np.cumsum([0] + sizes)
    bias_in, bias_out, bias_up, bias_down, gain_attn, shift_attn, gain_ff, shift_ff = (
        gathered[:, :, edges[i] : edges[i + 1]].reshape(-1).astype(full) for i in range(8)
    )
    norms = jnp.stack([gain_attn, shift_attn, gain_ff, shift_ff], 0)

    in_split = input_weight.reshape(shard, 3, seq, groups, lanes)
    up_split = up_weight.reshape(shard, dp, seq, units)
    out_split = output_weight.reshape(shard, seq, span)

    def head_piece(spot):
        mixed = jnp.swapaxes(pick(in_split, spot, 2), 1, 2).reshape(shard, 3 * span)
        return jnp.concatenate([mixed, pick(out_split, spot, 1)], 1)

    def unit_piece(spot):
        return pick(up_split, spot, 2).reshape(shard, dp * units)

    tokens_all = at.seq_gather(tokens)
    head_rows = place_at(at.seq_exchange(head_piece), at.seq_spots(), 0)
    head_all = at.dp_gather(head_rows.reshape(seq * shard, 4 * span)).reshape(width, 4 * span)
    unit_rows = place_at(at.seq_exchange(unit_piece), at.seq_spots(), 0)
    up_all = at.dp_gather(unit_rows.reshape(seq * shard, dp * units)).reshape(width, dp * units)
    down_all = at.dp_gather(down_weight).reshape(dp * units, width)
    in_all = head_all[:, : 3 * span]
    out_split_all = head_all[:, 3 * span :].reshape(seq, span, span)
    out_all = place_at(
        at.seq_exchange(lambda spot: pick(out_split_all, spot, 0)), at.seq_spots(), 1
    ).reshape(span, width)
    cot_all = at.seq_gather(cotangent)

    rows = seq * seqs * block
    x = jnp.stack(tokens_all, 0).reshape(rows, width)
    cot = jnp.stack(cot_all, 0).reshape(rows, width)

    in_bias_mine = jnp.swapaxes(
        pick(bias_in.reshape(3, seq, groups, lanes), rank, 1), 0, 1
    ).reshape(1, 3 * span)
    up_bias_mine = pick(bias_up.reshape(dp, seq, units), rank, 1).reshape(dp * units)

    cos_table, sin_table = rotary_tables(seq * block, lanes, head_dim)
    normed_attn, normed_ff, qkv = project(
        place, x, in_all, in_bias_mine, norms, jnp.asarray(cos_table), jnp.asarray(sin_table),
        block, seqs, lanes, head_dim,
    )
    qkv = qkv.reshape(seq, seqs, block, 3 * span)
    exact, attended, lse = attend(place, qkv, pair, head_dim)
    attended = attended.reshape(rows, span)

    hidden = jnp.dot(normed_ff, up_all, preferred_element_type=full) + up_bias_mine
    tail = 0.5 * (1.0 + lax.erf(hidden * np.float32(math.sqrt(0.5))))
    bell = jnp.exp(-0.5 * hidden * hidden) * np.float32(1.0 / math.sqrt(2.0 * math.pi))
    active = (hidden * tail).astype(low)
    slope = (tail + hidden * bell).astype(low)

    out_part = jnp.dot(attended, out_all, preferred_element_type=full) + jnp.dot(
        active, down_all, preferred_element_type=full
    )
    out_part = out_part.reshape(seq, seqs, block, width)
    out_sum = at.seq_reduce([out_part[k] for k in range(seq)])
    output = (tokens.astype(full) + out_sum + (bias_out + bias_down)).astype(low)

    attended_grad = contract(cot, out_all, 1, 1).astype(low)
    hidden_grad = (contract(cot, down_all, 1, 1) * slope.astype(full)).astype(low)
    down_grad = contract(active, cot, 0, 0)
    out_grad = contract(attended, cot, 0, 0)
    up_grad = contract(normed_ff, hidden_grad, 0, 0)

    order = [rank ^ k for k in range(seq)]
    tables = [
        jnp.stack([pick(jnp.asarray(t.reshape(seq, block, lanes)), spot, 0) for spot in order], 0)
        for t in (cos_table, sin_table)
    ]
    mixed_grad = attend_back(
        place, qkv, exact, attended_grad.reshape(seq, seqs, block, span), lse, *tables, pair, head_dim
    ).reshape(rows, 3 * span)
    in_grad = contract(normed_attn, mixed_grad, 0, 0)
    unit_grad, norm_sums = unproject(x, mixed_grad, hidden_grad, in_all, up_all, norms, block)
    unit_grad = unit_grad.reshape(seq, seqs, block, width)
    unit_sum = at.seq_reduce([unit_grad[k] for k in range(seq)])
    unit, rstd = normalised(tokens.astype(full))
    token_grad = cotangent.astype(full) + rstd * (
        unit_sum
        - jnp.mean(unit_sum, axis=-1, keepdims=True)
        - unit * jnp.mean(unit_sum * unit, axis=-1, keepdims=True)
    )
    token_grad = token_grad.astype(low)

    down_sum = at.dp_reduce(down_grad.reshape(dp, units, width))
    out_pieces = out_grad.astype(low).reshape(span, seq, span)
    out_grad = place_at(
        at.seq_exchange(lambda spot: pick(out_pieces, spot, 1)), at.seq_spots(), 0
    )
    out_sum_rows = at.dp_reduce(out_grad.reshape(dp, seq * shard, span))
    up_sum = at.dp_reduce(up_grad.reshape(dp, seq * shard, dp * units))
    in_sum = at.dp_reduce(in_grad.reshape(dp, seq * shard, 3 * span))

    def hand_back(total):
        split = total.reshape(seq, shard, total.shape[1]).astype(low)
        return [p.astype(full) for p in at.seq_exchange(lambda spot: pick(split, spot, 0))]

    up_final = place_at(
        [p.reshape(shard, dp, units) for p in hand_back(up_sum)], at.seq_spots(), 2
    ).reshape(shard, dp * seq * units)
    out_final = place_at(hand_back(out_sum_rows), at.seq_spots(), 1).reshape(shard, width)
    in_final = place_at(
        [
            jnp.swapaxes(p.reshape(shard, groups, 3, lanes), 1, 2).reshape(shard, 3, span)
            for p in hand_back(in_sum)
        ],
        at.seq_spots(),
        2,
    ).reshape(shard, 3 * width)

    in_bias_sum = jnp.sum(mixed_grad.astype(full), axis=0).reshape(groups, 3, lanes)
    in_bias_sum = jnp.swapaxes(in_bias_sum, 0, 1).reshape(3, 1, span)
    in_bias_sum = lax.dynamic_update_slice_in_dim(jnp.zeros((3, seq, span), full), in_bias_sum, rank, 1)
    up_bias_sum = jnp.sum(hidden_grad.astype(full), axis=0).reshape(dp, 1, units)
    up_bias_sum = lax.dynamic_update_slice_in_dim(jnp.zeros((dp, seq, units), full), up_bias_sum, rank, 1)
    out_bias_sum = jnp.sum(cotangent.astype(full), axis=(0, 1))
    in_bias_sum = in_bias_sum.reshape(3 * width)
    small = [
        in_bias_sum[: 2 * width],
        in_bias_sum[2 * width :],
        out_bias_sum,
        up_bias_sum,
        norm_sums[0],
        norm_sums[1],
        norm_sums[2],
        norm_sums[3],
    ]
    small = [v.reshape(dp, seq, -1) for v in small]
    edges = np.cumsum([0] + [v.shape[2] for v in small])
    total = at.small_reduce(jnp.concatenate(small, 2))
    (query_key_bias, value_bias, out_bias, up_bias_grad, *norm_grads) = [
        total[edges[i] : edges[i + 1]] for i in range(8)
    ]
    return (
        output,
        token_grad,
        in_final,
        query_key_bias,
        value_bias,
        out_final,
        out_bias,
        up_final,
        up_bias_grad,
        down_sum,
        out_bias,
        *norm_grads,
    )


def solution(mesh):
    rows = P(("dp", "seq"), None)
    flat = P(("dp", "seq"))
    held = P("dp", "seq", None)
    return jax.shard_map(
        on_device,
        mesh=mesh,
        in_specs=(held, rows, flat, rows, flat, rows, flat, rows, flat, flat, flat, flat, flat, held),
        out_specs=(held, held, rows, flat, flat, rows, flat, rows, flat, rows, flat, flat, flat, flat, flat),
        check_vma=False,
    )
```

time: 1670 us -> 581 us (0.35)
  waiting for transfers between devices: 1030 us -> 108 us
  blocking collectives: 310 us -> 0 us
  starting transfers between devices: 1.04 us -> 179 us
  matrix products: 156 us -> 56 us
  Pallas kernels: 0 us -> 77.4 us
    reduce_scatter x5 -> x0, waiting for transfers between devices: 885 us -> none  [the longest x1 362 us: on_device(): lax.psum_scatter(down_weight_grad, ('dp', 'seq'), scatter_dimension=0, ti...]
    all_gather x1 -> x0, blocking collectives: 229 us -> none  [on_device(): lax.all_gather(up_bias, ('dp', 'seq'), axis=0, tiled=True)]
    ppermute x0 -> x108, starting transfers between devices: none -> 179 us  [the longest x42 113 us: z_shift(): return lax.ppermute(array, 'dp', pairs)]
    all_gather x6 -> x0, waiting for transfers between devices: 143 us -> none  [the longest x1 48 us: on_device(): lax.all_gather(key_flat, 'seq', axis=1, tiled=True)]
    ppermute x0 -> x108, waiting for transfers between devices: none -> 108 us  [the longest x51 56.6 us: seq_swap(): return lax.ppermute(array, 'seq', [(i, i ^ k) for i in range(self.seq)])]
    dot_general x19 -> x9, matrix products: 156 us -> 56 us  [the longest x6 33.2 us: contract(): lax.dot_general(a, b, (((da,), (db,)), ((), ())), preferred_element_type=...]
    unnamed x2 -> x0, blocking collectives: 81.3 us -> none
    pallas_call x0 -> x4, Pallas kernels: none -> 77.4 us  [the longest x1 33.1 us: attend_back(): pl.pallas_call(functools.partial(attend_back_kernel, pair, head_dim), gri...]
  transfers between devices with their start and end apart: 11 -> 108, of which waited for: 7 -> 31; matrix products, arithmetic and copies ran while one was open for 17% -> 33% of each run, Pallas kernels for 0% -> 14%
where the time goes in v1:
time: 581 us; the launch traced here: 571 us
  starting transfers between devices  179 us (31%)
  waiting for transfers between devices  108 us (19%)
  local copies, waits for them, and re-layouts  103 us (18%)
  Pallas kernels  77.4 us (13%)
  matrix products  56 us (10%)
  other arithmetic  45.2 us (8%)
    ppermute x42, starting transfers between devices, z_shift(): return lax.ppermute(array, 'dp', pairs)  113 us
    ppermute x51, starting transfers between devices, seq_swap(): return lax.ppermute(array, 'seq', [(i, i ^ k) for i in range(self.seq)])  56.8 us
    ppermute x51, waiting for transfers between devices, seq_swap(): return lax.ppermute(array, 'seq', [(i, i ^ k) for i in range(self.seq)])  56.6 us
    ppermute x42, waiting for transfers between devices, z_shift(): return lax.ppermute(array, 'dp', pairs)  40.6 us
    dot_general x6, matrix products, contract(): lax.dot_general(a, b, (((da,), (db,)), ((), ())), preferred_element_type=...  33.2 us
    pallas_call x1, Pallas kernels, attend_back(): pl.pallas_call(functools.partial(attend_back_kernel, pair, head_dim), gri...  33.1 us
    dynamic_update_slice x37, local copies, waits for them, and re-layouts, place_at(): held = lax.dynamic_update_index_in_dim(held, piece, spot, axis)  30.2 us
    pallas_call x1, Pallas kernels, attend(): pl.pallas_call(functools.partial(attend_kernel, pair, head_dim), grid_spe...  18.3 us
  transfers between devices with their start and end apart: 108, of which 31 were waited for; matrix products, arithmetic and copies ran while one was open for 33% of the time, Pallas kernels for 14%

profile of v1, /device:TPU:0, one launch (start us, length us, event | category | flops | bytes accessed | tf_op | source)
XLA Modules:
  0.0 571.3 jit_solution(3781363600008857123)
XLA Ops:
  0.7 5.5 concatenate.59
  6.2 3.9 collective-permute-start.18
  35.5 3.8 collective-permute-done.20
  40.1 3.7 collective-permute-done.21
  61.9 4.2 collective-permute-done.39
  73.8 8.9 %collective-permute-done.52 = bf16[1,256,1024]{2,1,0:T(8,128)(2,1)} collective-permute-done((bf16[1,256,1024]{2,1,0:T(8,128)(2,1)}, bf16[1,256,1024]{2,1,0:T(8,128)(2,1)}, u32[]{:S(2)}, u32[]{:S(2)}) %collective-permute-start.52) | collective-permute-done | bytes 524320 | tf_op jit(solution)/shard_map/ppermute | solution.py:48
  84.4 4.6 collective-permute-start.37
  93.3 5.7 collective-permute-start.29
  100.3 6.2 %collective-permute-start.9 = (bf16[128,1024]{1,0:T(8,128)(2,1)S(1)}, bf16[128,1024]{1,0:T(8,128)(2,1)S(1)}, u32[]{:S(2)}, u32[]{:S(2)}) collective-permute-start(bf16[128,1024]{1,0:T(8,128)(2,1)S(1)} %bitcast.489), channel_id=1, source_target_pairs={{0,8},{4,12},{8,16},{12,20},{16,24},{20,28},{1,9},{5,13},{9,17},{1... | collective-permute-start | bytes 786440 | tf_op jit(solution)/shard_map/ppermute | solution.py:56
  107.8 4.9 collective-permute-start.38
  114.4 4.6 collective-permute-start.30
  120.3 4.6 collective-permute-start.10
  127.3 3.6 collective-permute-done.10
  133.1 4.0 collective-permute-start.11
  141.0 4.4 collective-permute-start.31
  150.9 7.4 %collective-permute-done.14 = bf16[128,1024]{1,0:T(8,128)(2,1)S(1)} collective-permute-done((bf16[128,1024]{1,0:T(8,128)(2,1)S(1)}, bf16[128,1024]{1,0:T(8,128)(2,1)S(1)}, u32[]{:S(2)}, u32[]{:S(2)}) %collective-permute-start.14) | collective-permute-done | bytes 262176 | tf_op jit(solution)/shard_map/ppermute | solution.py:56
  162.1 5.4 collective-permute-done.5
  183.0 11.5 %project.1 = (bf16[2048,1024]{1,0:T(8,128)(2,1)}, bf16[2048,1024]{1,0:T(8,128)(2,1)}, bf16[2048,768]{1,0:T(8,128)(2,1)}) custom-call(s32[1]{0:T(128)} %bitcast.place, bf16[2048,1024]{1,0:T(8,128)(2,1)} %bitcast.452, bf16[1024,768]{1,0:T(8,128)(2,1)} %slice.208.weight_ref.in_ref, f32[1,768]{1,0:T(1,128)} %reshape.388.bias_ref, ...), custom_call_target="tpu_custom_call" | custom-call | tf_op jit(solution)/shard_map/project/pallas_call | solution.py:226
  194.5 6.5 %copy.148 = bf16[1024,2048]{1,0:T(8,128)(2,1)} copy(bf16[1024,2048]{0,1:T(8,128)(2,1)} %bitcast.473) | data formatting | bytes 8388608 | tf_op jit(solution)/shard_map/dot_general | solution.py:256
  201.0 18.3 %attend.1 = (f32[4,1,512,256]{3,2,1,0:T(8,128)}, bf16[4,1,512,256]{3,2,1,0:T(8,128)(2,1)}, f32[4,1,2,2,512]{4,3,2,1,0:T(2,128)}) custom-call(s32[1]{0:T(128)} %bitcast.place, bf16[4,1,512,768]{3,2,1,0:T(8,128)(2,1)} %bitcast.464), custom_call_target="tpu_custom_call" | custom-call | tf_op jit(solution)/shard_map/attend/pallas_call | solution.py:310
  219.3 3.8 fusion.34
  232.1 8.2 %fusion.8 = (bf16[1024,2048]{0,1:T(8,128)(2,1)}, f32[2048,1024]{1,0:T(8,128)}) fusion(f32[1024]{0:T(1024)S(1)} %bitcast.527, bf16[2048,1024]{1,0:T(8,128)(2,1)S(1)} %copy-done.29, bf16[1024,1024]{1,0:T(8,128)(2,1)S(1)} %bitcast.469), kind=kOutput, calls=%fused_computation.15 | convolution fusion | flops 4307550208 | bytes 18878464 | tf_op jit(solution)/shard_map/dot_general | solution.py:536
  240.3 6.5 %copy.153 = bf16[1024,2048]{1,0:T(8,128)(2,1)} copy(bf16[1024,2048]{0,1:T(8,128)(2,1)} %get-tuple-element.140) | data formatting | bytes 8388608 | tf_op jit(solution)/shard_map/dot_general | solution.py:256
  246.8 7.7 %fusion.96 = f32[4,2,128,1024]{3,2,1,0:T(8,128)S(1)} fusion(bf16[4,2,128,2048]{3,2,1,0:T(8,128)(2,1)} %bitcast.474, bf16[2048,1024,1,1]{1,0,3,2:T(8,128)(2,1)} %bitcast.457), kind=kOutput, calls=%fused_computation.312 | convolution fusion | flops 4294967296 | bytes 12582912 | tf_op jit(solution)/shard_map/dot_general | solution.py:256
  257.6 6.5 %fusion.9 = f32[2048,1024]{1,0:T(8,128)} fusion(bf16[1024,1024]{1,0:T(8,128)(2,1)S(1)} %bitcast.479, f32[2048,1024]{1,0:T(8,128)S(1)} %copy-done.31, f32[1024]{0:T(1024)S(1)} %bitcast.528), kind=kOutput, calls=%fused_computation.18 | convolution fusion | flops 4307550208 | bytes 18878464 | tf_op jit(solution)/shard_map/dot_general | solution.py:542
  264.1 7.8 %convert_reduce_fusion = (f32[1024]{0:T(1024)S(1)}, bf16[2048,1024]{1,0:T(8,128)(2,1)S(1)}) fusion(f32[2048,1024]{1,0:T(8,128)S(1)} %copy-done.31, f32[1024]{0:T(1024)S(1)} %bitcast.529, bf16[2048,1024]{1,0:T(8,128)(2,1)S(1)} %bitcast.459, bf16[1024,1024]{1,0:T(8,128)(2,1)S(1)} %bitcast.480), kind=kOutput, calls=%fused_computation.11 | convolution fusion | flops 4326423552 | bytes 18882560 | tf_op jit(solution)/shard_map/dot_general | solution.py:256
  272.0 6.2 %fusion.95 = f32[1024,1024]{1,0:T(8,128)} fusion(bf16[2048,1024]{1,0:T(8,128)(2,1)S(1)} %copy-done.30, bf16[2048,1024]{1,0:T(8,128)(2,1)S(1)} %get-tuple-element.139.hidden_ref), kind=kOutput, calls=%fused_computation.311 | convolution fusion | flops 4294967296 | bytes 12582912 | tf_op jit(solution)/shard_map/dot_general | solution.py:256
  284.3 4.4 convolution_convert_fusion
  290.4 33.1 %attend_back.1 = bf16[4,1,512,768]{3,2,1,0:T(8,128)(2,1)} custom-call(s32[1]{0:T(128)} %bitcast.place, bf16[4,1,512,768]{3,2,1,0:T(8,128)(2,1)} %bitcast.465, f32[4,1,512,256]{3,2,1,0:T(8,128)} %get-tuple-element.26.exact_ref, bf16[4,1,512,256]{3,2,1,0:T(8,128)(2,1)} %bitcast.486, f32[4,1,2,2,512]{4,3,2,1,0:T(2,128)} %get-tuple-element.27.lse_ref, ...), custom_call_target="tpu_custom_call" | custom-call | tf_op jit(solution)/shard_map/attend_back/pallas_call | solution.py:388
  323.6 14.4 %unproject.1 = (f32[2048,1024]{1,0:T(8,128)}, f32[4,1024]{1,0:T(4,128)}) custom-call(bf16[2048,1024]{1,0:T(8,128)(2,1)} %bitcast.453, bf16[2048,768]{1,0:T(8,128)(2,1)} %bitcast.455, bf16[2048,1024]{1,0:T(8,128)(2,1)} %copy-done.10, bf16[1024,768]{1,0:T(8,128)(2,1)} %slice.208.weight_ref.in_ref, bf16[1024,1024]{1,0:T(8,128)(2,1)} %bitcast.470, ...), custom_call_target="tpu_custom_call" | custom-call | tf_op jit(solution)/shard_map/unproject/pallas_call | solution.py:434
  338.0 8.1 %fusion.93 = (bf16[2048,1024]{1,0:T(8,128)(2,1)S(1)}, f32[2048,1024]{1,0:T(8,128)}) fusion(f32[2048,1024]{1,0:T(8,128)} %fusion.9, bf16[2048,256]{1,0:T(8,128)(2,1)S(1)} %bitcast.471, bf16[256,1024]{0,1:T(8,128)(2,1)S(1)} %bitcast.478), kind=kOutput, calls=%fused_computation.309 | convolution fusion | flops 1077936128 | bytes 22544384 | tf_op jit(solution)/shard_map/dot_general | solution.py:542
  354.6 3.4 fusion.94
  359.8 3.9 collective-permute-start.82
  366.7 3.2 collective-permute-done.85
  369.9 3.9 collective-permute-start.83
  376.2 3.8 collective-permute-done.86
  383.9 4.3 collective-permute-done.87
  405.3 10.8 %collective-permute-done.56 = bf16[1,256,1024]{2,1,0:T(8,128)(2,1)S(1)} collective-permute-done((bf16[1,256,1024]{2,1,0:T(8,128)(2,1)}, bf16[1,256,1024]{2,1,0:T(8,128)(2,1)S(1)}, u32[]{:S(2)}, u32[]{:S(2)}) %collective-permute-start.56) | collective-permute-done | bytes 524320 | tf_op jit(solution)/shard_map/ppermute | solution.py:48
  430.0 4.8 collective-permute-done.55
  435.4 16.9 %collective-permute-done.57 = bf16[1,256,1024]{2,1,0:T(8,128)(2,1)S(1)} collective-permute-done((bf16[1,256,1024]{2,1,0:T(8,128)(2,1)S(1)}, bf16[1,256,1024]{2,1,0:T(8,128)(2,1)S(1)}, u32[]{:S(2)}, u32[]{:S(2)}) %collective-permute-start.57) | collective-permute-done | bytes 524320 | tf_op jit(solution)/shard_map/ppermute | solution.py:48
  458.8 6.2 %collective-permute-done.45 = bf16[1,256,1024]{2,1,0:T(8,128)(2,1)S(1)} collective-permute-done((bf16[1,256,1024]{2,1,0:T(8,128)(2,1)S(1)}, bf16[1,256,1024]{2,1,0:T(8,128)(2,1)S(1)}, u32[]{:S(2)}, u32[]{:S(2)}) %collective-permute-start.45) | collective-permute-done | bytes 524320 | tf_op jit(solution)/shard_map/ppermute | solution.py:48
  466.8 3.9 convert_reduce_fusion.3
  489.2 5.0 collective-permute-start.63
  497.4 5.2 collective-permute-start.103
  504.1 4.6 collective-permute-start.64
  510.1 4.6 collective-permute-start.93
  519.0 3.9 collective-permute-done.96
  544.2 4.6 collective-permute-start.104
  (513 shorter events, 247.0 us)
Async XLA Ops:
  6.2 25.7 %collective-permute-start.18 = (bf16[512]{0:T(512)(128)(2,1)S(1)}, bf16[512]{0:T(512)(128)(2,1)}, u32[]{:S(2)}, u32[]{:S(2)}) collective-permute-start(bf16[512]{0:T(512)(128)(2,1)S(1)} %concatenate.59), channel_id=1, source_target_pairs={{0,3},{1,2},{2,1},{3,0},{4,7},{5,6},{6,5},{7,4},{8,11},{9,10},{10,... | collective-permute-start | bytes 3080 | tf_op jit(solution)/shard_map/ppermute | solution.py:48
  10.1 19.1 %collective-permute-start.17 = (bf16[512]{0:T(512)(128)(2,1)S(1)}, bf16[512]{0:T(512)(128)(2,1)}, u32[]{:S(2)}, u32[]{:S(2)}) collective-permute-start(bf16[512]{0:T(512)(128)(2,1)S(1)} %concatenate.59), channel_id=1, source_target_pairs={{0,2},{1,3},{2,0},{3,1},{4,6},{5,7},{6,4},{7,5},{8,10},{9,11},{10,... | collective-permute-start | bytes 3080 | tf_op jit(solution)/shard_map/ppermute | solution.py:48
  10.6 17.7 %collective-permute-start.16 = (bf16[512]{0:T(512)(128)(2,1)S(1)}, bf16[512]{0:T(512)(128)(2,1)}, u32[]{:S(2)}, u32[]{:S(2)}) collective-permute-start(bf16[512]{0:T(512)(128)(2,1)S(1)} %concatenate.59), channel_id=1, source_target_pairs={{0,1},{1,0},{2,3},{3,2},{4,5},{5,4},{6,7},{7,6},{8,9},{9,8},{10,11... | collective-permute-start | bytes 3080 | tf_op jit(solution)/shard_map/ppermute | solution.py:48
  13.8 41.1 %collective-permute-start.7 = (bf16[32,1024]{1,0:T(8,128)(2,1)}, bf16[32,1024]{1,0:T(8,128)(2,1)S(1)}, u32[]{:S(2)}, u32[]{:S(2)}) collective-permute-start(bf16[32,1024]{1,0:T(8,128)(2,1)} %pad_maximum_fusion.5), channel_id=1, source_target_pairs={{0,2},{1,3},{2,0},{3,1},{4,6},{5,7},{6,4},{7,5},{8,10},{9,11},{10,... | collective-permute-start | bytes 196616 | tf_op jit(solution)/shard_map/ppermute | solution.py:48
  16.5 39.7 %collective-permute-start.8 = (bf16[32,1024]{1,0:T(8,128)(2,1)}, bf16[32,1024]{1,0:T(8,128)(2,1)}, u32[]{:S(2)}, u32[]{:S(2)}) collective-permute-start(bf16[32,1024]{1,0:T(8,128)(2,1)} %pad_maximum_fusion.6), channel_id=1, source_target_pairs={{0,3},{1,2},{2,1},{3,0},{4,7},{5,6},{6,5},{7,4},{8,11},{9,10},{10,... | collective-permute-start | bytes 196616 | tf_op jit(solution)/shard_map/ppermute | solution.py:48
  28.3 29.0 %collective-permute-start.6 = (bf16[32,1024]{1,0:T(8,128)(2,1)S(1)}, bf16[32,1024]{1,0:T(8,128)(2,1)S(1)}, u32[]{:S(2)}, u32[]{:S(2)}) collective-permute-start(bf16[32,1024]{1,0:T(8,128)(2,1)S(1)} %copy-done.25), channel_id=1, source_target_pairs={{0,1},{1,0},{2,3},{3,2},{4,5},{5,4},{6,7},{7,6},{8,9},{9,8},{10,11... | collective-permute-start | bytes 196616 | tf_op jit(solution)/shard_map/ppermute | solution.py:48
  29.3 21.0 %collective-permute-start.26 = (bf16[32,1024]{1,0:T(8,128)(2,1)}, bf16[32,1024]{1,0:T(8,128)(2,1)}, u32[]{:S(2)}, u32[]{:S(2)}) collective-permute-start(bf16[32,1024]{1,0:T(8,128)(2,1)} %bitcast.516), channel_id=1, source_target_pairs={{0,1},{1,0},{2,3},{3,2},{4,5},{5,4},{6,7},{7,6},{8,9},{9,8},{10,11... | collective-permute-start | bytes 196616 | tf_op jit(solution)/shard_map/ppermute | solution.py:48
  58.6 24.0 %collective-permute-start.52 = (bf16[1,256,1024]{2,1,0:T(8,128)(2,1)}, bf16[1,256,1024]{2,1,0:T(8,128)(2,1)}, u32[]{:S(2)}, u32[]{:S(2)}) collective-permute-start(bf16[1,256,1024]{2,1,0:T(8,128)(2,1)} %get-tuple-element.81), channel_id=1, source_target_pairs={{0,2},{1,3},{2,0},{3,1},{4,6},{5,7},{6,4},{7,5},{8,10},{9,11},{10,... | collective-permute-start | bytes 1572872 | tf_op jit(solution)/shard_map/ppermute | solution.py:48
  66.1 18.3 %collective-permute-start.50 = (bf16[1,256,1024]{2,1,0:T(8,128)(2,1)}, bf16[1,256,1024]{2,1,0:T(8,128)(2,1)S(1)}, u32[]{:S(2)}, u32[]{:S(2)}) collective-permute-start(bf16[1,256,1024]{2,1,0:T(8,128)(2,1)} %get-tuple-element.81), channel_id=1, source_target_pairs={{0,1},{1,0},{2,3},{3,2},{4,5},{5,4},{6,7},{7,6},{8,9},{9,8},{10,11... | collective-permute-start | bytes 1572872 | tf_op jit(solution)/shard_map/ppermute | solution.py:48
  68.8 30.2 %collective-permute-start.2 = (bf16[1,256,1024]{2,1,0:T(8,128)(2,1)}, bf16[1,256,1024]{2,1,0:T(8,128)(2,1)S(1)}, u32[]{:S(2)}, u32[]{:S(2)}) collective-permute-start(bf16[1,256,1024]{2,1,0:T(8,128)(2,1)} %get-tuple-element.84), channel_id=1, source_target_pairs={{0,2},{1,3},{2,0},{3,1},{4,6},{5,7},{6,4},{7,5},{8,10},{9,11},{10,... | collective-permute-start | bytes 1572872 | tf_op jit(solution)/shard_map/ppermute | solution.py:48
  71.4 28.9 %collective-permute-start = (bf16[1,256,1024]{2,1,0:T(8,128)(2,1)}, bf16[1,256,1024]{2,1,0:T(8,128)(2,1)S(1)}, u32[]{:S(2)}, u32[]{:S(2)}) collective-permute-start(bf16[1,256,1024]{2,1,0:T(8,128)(2,1)} %get-tuple-element.84), channel_id=1, source_target_pairs={{0,1},{1,0},{2,3},{3,2},{4,5},{5,4},{6,7},{7,6},{8,9},{9,8},{10,11... | collective-permute-start | bytes 1572872 | tf_op jit(solution)/shard_map/ppermute | solution.py:48
  72.5 34.0 %collective-permute-start.3 = (bf16[1,256,1024]{2,1,0:T(8,128)(2,1)S(1)}, bf16[1,256,1024]{2,1,0:T(8,128)(2,1)S(1)}, u32[]{:S(2)}, u32[]{:S(2)}) collective-permute-start(bf16[1,256,1024]{2,1,0:T(8,128)(2,1)S(1)} %get-tuple-element.85), channel_id=1, source_target_pairs={{0,2},{1,3},{2,0},{3,1},{4,6},{5,7},{6,4},{7,5},{8,10},{9,11},{10,... | collective-permute-start | bytes 1572872 | tf_op jit(solution)/shard_map/ppermute | solution.py:48
  82.7 25.1 %collective-permute-start.1 = (bf16[1,256,1024]{2,1,0:T(8,128)(2,1)S(1)}, bf16[1,256,1024]{2,1,0:T(8,128)(2,1)S(1)}, u32[]{:S(2)}, u32[]{:S(2)}) collective-permute-start(bf16[1,256,1024]{2,1,0:T(8,128)(2,1)S(1)} %get-tuple-element.85), channel_id=1, source_target_pairs={{0,1},{1,0},{2,3},{3,2},{4,5},{5,4},{6,7},{7,6},{8,9},{9,8},{10,11... | collective-permute-start | bytes 1572872 | tf_op jit(solution)/shard_map/ppermute | solution.py:48
  93.3 19.6 %collective-permute-start.29 = (bf16[128,1024]{1,0:T(8,128)(2,1)S(1)}, bf16[128,1024]{1,0:T(8,128)(2,1)S(1)}, u32[]{:S(2)}, u32[]{:S(2)}) collective-permute-start(bf16[128,1024]{1,0:T(8,128)(2,1)S(1)} %bitcast.492), channel_id=1, source_target_pairs={{0,8},{4,12},{8,16},{12,20},{16,24},{20,28},{1,9},{5,13},{9,17},{1... | collective-permute-start | bytes 786440 | tf_op jit(solution)/shard_map/ppermute | solution.py:56
  100.3 18.6 %collective-permute-start.9 = (bf16[128,1024]{1,0:T(8,128)(2,1)S(1)}, bf16[128,1024]{1,0:T(8,128)(2,1)S(1)}, u32[]{:S(2)}, u32[]{:S(2)}) collective-permute-start(bf16[128,1024]{1,0:T(8,128)(2,1)S(1)} %bitcast.489), channel_id=1, source_target_pairs={{0,8},{4,12},{8,16},{12,20},{16,24},{20,28},{1,9},{5,13},{9,17},{1... | collective-permute-start | bytes 786440 | tf_op jit(solution)/shard_map/ppermute | solution.py:56
  112.9 32.6 %collective-permute-start.33 = (bf16[128,1024]{1,0:T(8,128)(2,1)S(1)}, bf16[128,1024]{1,0:T(8,128)(2,1)S(1)}, u32[]{:S(2)}, u32[]{:S(2)}) collective-permute-start(bf16[128,1024]{1,0:T(8,128)(2,1)S(1)} %collective-permute-done.32), channel_id=1, source_target_pairs={{8,0},{12,4},{16,8},{20,12},{24,16},{28,20},{9,1},{13,5},{17,9},{2... | collective-permute-start | bytes 786440 | tf_op jit(solution)/shard_map/ppermute | solution.py:56
  114.4 22.9 %collective-permute-start.30 = (bf16[128,1024]{1,0:T(8,128)(2,1)S(1)}, bf16[128,1024]{1,0:T(8,128)(2,1)S(1)}, u32[]{:S(2)}, u32[]{:S(2)}) collective-permute-start(bf16[128,1024]{1,0:T(8,128)(2,1)S(1)} %collective-permute-done.29), channel_id=1, source_target_pairs={{0,8},{4,12},{8,16},{12,20},{16,24},{20,28},{1,9},{5,13},{9,17},{1... | collective-permute-start | bytes 786440 | tf_op jit(solution)/shard_map/ppermute | solution.py:56
  119.0 28.2 %collective-permute-start.13 = (bf16[128,1024]{1,0:T(8,128)(2,1)S(1)}, bf16[128,1024]{1,0:T(8,128)(2,1)S(1)}, u32[]{:S(2)}, u32[]{:S(2)}) collective-permute-start(bf16[128,1024]{1,0:T(8,128)(2,1)S(1)} %collective-permute-done.12), channel_id=1, source_target_pairs={{8,0},{12,4},{16,8},{20,12},{24,16},{28,20},{9,1},{13,5},{17,9},{2... | collective-permute-start | bytes 786440 | tf_op jit(solution)/shard_map/ppermute | solution.py:56
  130.9 30.5 %collective-permute-start.53 = (bf16[1,256,1024]{2,1,0:T(8,128)(2,1)}, bf16[1,256,1024]{2,1,0:T(8,128)(2,1)S(1)}, u32[]{:S(2)}, u32[]{:S(2)}) collective-permute-start(bf16[1,256,1024]{2,1,0:T(8,128)(2,1)} %collective-permute-done.49), channel_id=1, source_target_pairs={{0,2},{1,3},{2,0},{3,1},{4,6},{5,7},{6,4},{7,5},{8,10},{9,11},{10,... | collective-permute-start | bytes 1572872 | tf_op jit(solution)/shard_map/ppermute | solution.py:48
  137.3 24.6 %collective-permute-start.54 = (bf16[1,256,1024]{2,1,0:T(8,128)(2,1)}, bf16[1,256,1024]{2,1,0:T(8,128)(2,1)S(1)}, u32[]{:S(2)}, u32[]{:S(2)}) collective-permute-start(bf16[1,256,1024]{2,1,0:T(8,128)(2,1)} %collective-permute-done.52), channel_id=1, source_target_pairs={{0,1},{1,0},{2,3},{3,2},{4,5},{5,4},{6,7},{7,6},{8,9},{9,8},{10,11... | collective-permute-start | bytes 1572872 | tf_op jit(solution)/shard_map/ppermute | solution.py:48
  161.9 66.4 %collective-permute-start.35 = (bf16[4,128,1024]{2,1,0:T(8,128)(2,1)}, bf16[4,128,1024]{2,1,0:T(8,128)(2,1)}, u32[]{:S(2)}, u32[]{:S(2)}) collective-permute-start(bf16[4,128,1024]{2,1,0:T(8,128)(2,1)} %constant_dynamic-slice_fusion.28), channel_id=1, source_target_pairs={{0,4},{4,0},{8,12},{12,8},{16,20},{20,16},{24,28},{28,24},{1,5},{5... | collective-permute-start | bytes 3145736 | tf_op jit(solution)/shard_map/ppermute | solution.py:51
  179.4 101.6 %collective-permute-start.23 = (bf16[256,256]{0,1:T(8,128)(2,1)}, bf16[256,256]{0,1:T(8,128)(2,1)}, u32[]{:S(2)}, u32[]{:S(2)}) collective-permute-start(bf16[256,256]{0,1:T(8,128)(2,1)} %bitcast.42), channel_id=1, source_target_pairs={{0,1},{1,0},{2,3},{3,2},{4,5},{5,4},{6,7},{7,6},{8,9},{9,8},{10,11... | collective-permute-start | bytes 393224 | tf_op jit(solution)/shard_map/ppermute | solution.py:48
  181.2 101.2 %collective-permute-start.24 = (bf16[256,256]{0,1:T(8,128)(2,1)}, bf16[256,256]{0,1:T(8,128)(2,1)}, u32[]{:S(2)}, u32[]{:S(2)}) collective-permute-start(bf16[256,256]{0,1:T(8,128)(2,1)} %bitcast.44), channel_id=1, source_target_pairs={{0,2},{1,3},{2,0},{3,1},{4,6},{5,7},{6,4},{7,5},{8,10},{9,11},{10,... | collective-permute-start | bytes 393224 | tf_op jit(solution)/shard_map/ppermute | solution.py:48
  182.5 100.9 %collective-permute-start.25 = (bf16[256,256]{0,1:T(8,128)(2,1)}, bf16[256,256]{0,1:T(8,128)(2,1)}, u32[]{:S(2)}, u32[]{:S(2)}) collective-permute-start(bf16[256,256]{0,1:T(8,128)(2,1)} %bitcast.46), channel_id=1, source_target_pairs={{0,3},{1,2},{2,1},{3,0},{4,7},{5,6},{6,5},{7,4},{8,11},{9,10},{10,... | collective-permute-start | bytes 393224 | tf_op jit(solution)/shard_map/ppermute | solution.py:48
  226.6 62.1 %collective-permute-start.78 = (bf16[256,256]{1,0:T(8,128)(2,1)}, bf16[256,256]{1,0:T(8,128)(2,1)S(1)}, u32[]{:S(2)}, u32[]{:S(2)}) collective-permute-start(bf16[256,256]{1,0:T(8,128)(2,1)} %bitcast.437), channel_id=1, source_target_pairs={{0,1},{1,0},{2,3},{3,2},{4,5},{5,4},{6,7},{7,6},{8,9},{9,8},{10,11... | collective-permute-start | bytes 393224 | tf_op jit(solution)/shard_map/ppermute | solution.py:48
  228.3 60.4 %collective-permute-start.79 = (bf16[256,256]{1,0:T(8,128)(2,1)}, bf16[256,256]{1,0:T(8,128)(2,1)}, u32[]{:S(2)}, u32[]{:S(2)}) collective-permute-start(bf16[256,256]{1,0:T(8,128)(2,1)} %bitcast.436), channel_id=1, source_target_pairs={{0,2},{1,3},{2,0},{3,1},{4,6},{5,7},{6,4},{7,5},{8,10},{9,11},{10,... | collective-permute-start | bytes 393224 | tf_op jit(solution)/shard_map/ppermute | solution.py:48
  290.4 68.1 %collective-permute-start.81 = (bf16[4,128,256]{2,1,0:T(8,128)(2,1)}, bf16[4,128,256]{2,1,0:T(8,128)(2,1)}, u32[]{:S(2)}, u32[]{:S(2)}) collective-permute-start(bf16[4,128,256]{2,1,0:T(8,128)(2,1)} %dynamic-slice_bitcast_fusion), channel_id=1, source_target_pairs={{0,4},{4,0},{8,12},{12,8},{16,20},{20,16},{24,28},{28,24},{1,5},{5... | collective-permute-start | bytes 786440 | tf_op jit(solution)/shard_map/ppermute | solution.py:51
  348.5 53.1 %collective-permute-start.44 = (bf16[1,256,1024]{2,1,0:T(8,128)(2,1)}, bf16[1,256,1024]{2,1,0:T(8,128)(2,1)}, u32[]{:S(2)}, u32[]{:S(2)}) collective-permute-start(bf16[1,256,1024]{2,1,0:T(8,128)(2,1)} %get-tuple-element.82), channel_id=1, source_target_pairs={{0,1},{1,0},{2,3},{3,2},{4,5},{5,4},{6,7},{7,6},{8,9},{9,8},{10,11... | collective-permute-start | bytes 1572872 | tf_op jit(solution)/shard_map/ppermute | solution.py:48
  350.2 53.0 %collective-permute-start.46 = (bf16[1,256,1024]{2,1,0:T(8,128)(2,1)}, bf16[1,256,1024]{2,1,0:T(8,128)(2,1)}, u32[]{:S(2)}, u32[]{:S(2)}) collective-permute-start(bf16[1,256,1024]{2,1,0:T(8,128)(2,1)} %get-tuple-element.83), channel_id=1, source_target_pairs={{0,2},{1,3},{2,0},{3,1},{4,6},{5,7},{6,4},{7,5},{8,10},{9,11},{10,... | collective-permute-start | bytes 1572872 | tf_op jit(solution)/shard_map/ppermute | solution.py:48
  399.1 23.7 %collective-permute-start.101 = (bf16[4,128,1024]{2,1,0:T(8,128)(2,1)}, bf16[4,128,1024]{2,1,0:T(8,128)(2,1)}, u32[]{:S(2)}, u32[]{:S(2)}) collective-permute-start(bf16[4,128,1024]{2,1,0:T(8,128)(2,1)} %fusion.38), channel_id=1, source_target_pairs={{0,4},{4,0},{8,12},{12,8},{16,20},{20,16},{24,28},{28,24},{1,5},{5... | collective-permute-start | bytes 3145736 | tf_op jit(solution)/shard_map/ppermute | solution.py:51
  399.4 26.9 %collective-permute-start.91 = (bf16[4,128,1024]{2,1,0:T(8,128)(2,1)}, bf16[4,128,1024]{2,1,0:T(8,128)(2,1)}, u32[]{:S(2)}, u32[]{:S(2)}) collective-permute-start(bf16[4,128,1024]{2,1,0:T(8,128)(2,1)} %fusion.37), channel_id=1, source_target_pairs={{0,4},{4,0},{8,12},{12,8},{16,20},{20,16},{24,28},{28,24},{1,5},{5... | collective-permute-start | bytes 3145736 | tf_op jit(solution)/shard_map/ppermute | solution.py:51
  400.2 19.5 %collective-permute-start.61 = (bf16[4,128,768]{2,1,0:T(8,128)(2,1)S(1)}, bf16[4,128,768]{2,1,0:T(8,128)(2,1)}, u32[]{:S(2)}, u32[]{:S(2)}) collective-permute-start(bf16[4,128,768]{2,1,0:T(8,128)(2,1)S(1)} %fusion.40), channel_id=1, source_target_pairs={{0,4},{4,0},{8,12},{12,8},{16,20},{20,16},{24,28},{28,24},{1,5},{5... | collective-permute-start | bytes 2359304 | tf_op jit(solution)/shard_map/ppermute | solution.py:51
  416.1 49.0 %collective-permute-start.48 = (bf16[1,256,1024]{2,1,0:T(8,128)(2,1)}, bf16[1,256,1024]{2,1,0:T(8,128)(2,1)S(1)}, u32[]{:S(2)}, u32[]{:S(2)}) collective-permute-start(bf16[1,256,1024]{2,1,0:T(8,128)(2,1)} %slice.225), channel_id=1, source_target_pairs={{0,2},{1,3},{2,0},{3,1},{4,6},{5,7},{6,4},{7,5},{8,10},{9,11},{10,... | collective-permute-start | bytes 1572872 | tf_op jit(solution)/shard_map/ppermute | solution.py:48
  417.7 35.1 %collective-permute-start.60 = (bf16[1,256,1024]{2,1,0:T(8,128)(2,1)}, bf16[1,256,1024]{2,1,0:T(8,128)(2,1)S(1)}, u32[]{:S(2)}, u32[]{:S(2)}) collective-permute-start(bf16[1,256,1024]{2,1,0:T(8,128)(2,1)} %slice.236), channel_id=1, source_target_pairs={{0,2},{1,3},{2,0},{3,1},{4,6},{5,7},{6,4},{7,5},{8,10},{9,11},{10,... | collective-permute-start | bytes 1572872 | tf_op jit(solution)/shard_map/ppermute | solution.py:48
  423.3 29.0 %collective-permute-start.57 = (bf16[1,256,1024]{2,1,0:T(8,128)(2,1)S(1)}, bf16[1,256,1024]{2,1,0:T(8,128)(2,1)S(1)}, u32[]{:S(2)}, u32[]{:S(2)}) collective-permute-start(bf16[1,256,1024]{2,1,0:T(8,128)(2,1)S(1)} %add_convert_fusion.1), channel_id=1, source_target_pairs={{0,2},{1,3},{2,0},{3,1},{4,6},{5,7},{6,4},{7,5},{8,10},{9,11},{10,... | collective-permute-start | bytes 1572872 | tf_op jit(solution)/shard_map/ppermute | solution.py:48
  426.3 27.4 %collective-permute-start.59 = (bf16[1,256,1024]{2,1,0:T(8,128)(2,1)S(1)}, bf16[1,256,1024]{2,1,0:T(8,128)(2,1)S(1)}, u32[]{:S(2)}, u32[]{:S(2)}) collective-permute-start(bf16[1,256,1024]{2,1,0:T(8,128)(2,1)S(1)} %add_convert_fusion), channel_id=1, source_target_pairs={{0,1},{1,0},{2,3},{3,2},{4,5},{5,4},{6,7},{7,6},{8,9},{9,8},{10,11... | collective-permute-start | bytes 1572872 | tf_op jit(solution)/shard_map/ppermute | solution.py:48
  434.8 22.5 %collective-permute-start.43 = (bf16[1,256,1024]{2,1,0:T(8,128)(2,1)S(1)}, bf16[1,256,1024]{2,1,0:T(8,128)(2,1)S(1)}, u32[]{:S(2)}, u32[]{:S(2)}) collective-permute-start(bf16[1,256,1024]{2,1,0:T(8,128)(2,1)S(1)} %copy-done.19), channel_id=1, source_target_pairs={{0,1},{1,0},{2,3},{3,2},{4,5},{5,4},{6,7},{7,6},{8,9},{9,8},{10,11... | collective-permute-start | bytes 1572872 | tf_op jit(solution)/shard_map/ppermute | solution.py:48
  453.7 28.6 %collective-permute-start.62 = (bf16[128,768]{1,0:T(8,128)(2,1)}, bf16[128,768]{1,0:T(8,128)(2,1)}, u32[]{:S(2)}, u32[]{:S(2)}) collective-permute-start(bf16[128,768]{1,0:T(8,128)(2,1)} %get-tuple-element.65), channel_id=1, source_target_pairs={{0,8},{4,12},{8,16},{12,20},{16,24},{20,28},{1,9},{5,13},{9,17},{1... | collective-permute-start | bytes 589832 | tf_op jit(solution)/shard_map/ppermute | solution.py:56
  457.4 26.1 %collective-permute-start.65 = (bf16[128,768]{1,0:T(8,128)(2,1)}, bf16[128,768]{1,0:T(8,128)(2,1)}, u32[]{:S(2)}, u32[]{:S(2)}) collective-permute-start(bf16[128,768]{1,0:T(8,128)(2,1)} %get-tuple-element.66), channel_id=1, source_target_pairs={{8,0},{12,4},{16,8},{20,12},{24,16},{28,20},{9,1},{13,5},{17,9},{2... | collective-permute-start | bytes 589832 | tf_op jit(solution)/shard_map/ppermute | solution.py:56
  474.8 19.4 %collective-permute-start.102 = (bf16[128,1024]{1,0:T(8,128)(2,1)S(1)}, bf16[128,1024]{1,0:T(8,128)(2,1)S(1)}, u32[]{:S(2)}, u32[]{:S(2)}) collective-permute-start(bf16[128,1024]{1,0:T(8,128)(2,1)S(1)} %get-tuple-element.53), channel_id=1, source_target_pairs={{0,8},{4,12},{8,16},{12,20},{16,24},{20,28},{1,9},{5,13},{9,17},{1... | collective-permute-start | bytes 786440 | tf_op jit(solution)/shard_map/ppermute | solution.py:56
  476.8 18.8 %collective-permute-start.105 = (bf16[128,1024]{1,0:T(8,128)(2,1)S(1)}, bf16[128,1024]{1,0:T(8,128)(2,1)}, u32[]{:S(2)}, u32[]{:S(2)}) collective-permute-start(bf16[128,1024]{1,0:T(8,128)(2,1)S(1)} %get-tuple-element.54), channel_id=1, source_target_pairs={{8,0},{12,4},{16,8},{20,12},{24,16},{28,20},{9,1},{13,5},{17,9},{2... | collective-permute-start | bytes 786440 | tf_op jit(solution)/shard_map/ppermute | solution.py:56
  485.1 23.5 %collective-permute-start.92 = (bf16[128,1024]{1,0:T(8,128)(2,1)S(1)}, bf16[128,1024]{1,0:T(8,128)(2,1)S(1)}, u32[]{:S(2)}, u32[]{:S(2)}) collective-permute-start(bf16[128,1024]{1,0:T(8,128)(2,1)S(1)} %get-tuple-element.59), channel_id=1, source_target_pairs={{0,8},{4,12},{8,16},{12,20},{16,24},{20,28},{1,9},{5,13},{9,17},{1... | collective-permute-start | bytes 786440 | tf_op jit(solution)/shard_map/ppermute | solution.py:56
  487.9 22.0 %collective-permute-start.95 = (bf16[128,1024]{1,0:T(8,128)(2,1)S(1)}, bf16[128,1024]{1,0:T(8,128)(2,1)S(1)}, u32[]{:S(2)}, u32[]{:S(2)}) collective-permute-start(bf16[128,1024]{1,0:T(8,128)(2,1)S(1)} %get-tuple-element.60), channel_id=1, source_target_pairs={{8,0},{12,4},{16,8},{20,12},{24,16},{28,20},{9,1},{13,5},{17,9},{2... | collective-permute-start | bytes 786440 | tf_op jit(solution)/shard_map/ppermute | solution.py:56
  497.4 45.6 %collective-permute-start.103 = (bf16[128,1024]{1,0:T(8,128)(2,1)}, bf16[128,1024]{1,0:T(8,128)(2,1)}, u32[]{:S(2)}, u32[]{:S(2)}) collective-permute-start(bf16[128,1024]{1,0:T(8,128)(2,1)} %get-tuple-element.51), channel_id=1, source_target_pairs={{0,8},{4,12},{8,16},{12,20},{16,24},{20,28},{1,9},{5,13},{9,17},{1... | collective-permute-start | bytes 786440 | tf_op jit(solution)/shard_map/ppermute | solution.py:56
  502.7 40.4 %collective-permute-start.106 = (bf16[128,1024]{1,0:T(8,128)(2,1)}, bf16[128,1024]{1,0:T(8,128)(2,1)}, u32[]{:S(2)}, u32[]{:S(2)}) collective-permute-start(bf16[128,1024]{1,0:T(8,128)(2,1)} %get-tuple-element.52), channel_id=1, source_target_pairs={{8,0},{12,4},{16,8},{20,12},{24,16},{28,20},{9,1},{13,5},{17,9},{2... | collective-permute-start | bytes 786440 | tf_op jit(solution)/shard_map/ppermute | solution.py:56
  516.3 17.4 %collective-permute-start.70 = (bf16[32,768]{1,0:T(8,128)(2,1)S(1)}, bf16[32,768]{1,0:T(8,128)(2,1)S(1)}, u32[]{:S(2)}, u32[]{:S(2)}) collective-permute-start(bf16[32,768]{1,0:T(8,128)(2,1)S(1)} %get-tuple-element.104), channel_id=1, source_target_pairs={{0,3},{1,2},{2,1},{3,0},{4,7},{5,6},{6,5},{7,4},{8,11},{9,10},{10,... | collective-permute-start | bytes 147464 | tf_op jit(solution)/shard_map/ppermute | solution.py:48
  524.3 26.0 %collective-permute-start.94 = (bf16[128,1024]{1,0:T(8,128)(2,1)}, bf16[128,1024]{1,0:T(8,128)(2,1)S(1)}, u32[]{:S(2)}, u32[]{:S(2)}) collective-permute-start(bf16[128,1024]{1,0:T(8,128)(2,1)} %get-tuple-element.55), channel_id=1, source_target_pairs={{0,8},{4,12},{8,16},{12,20},{16,24},{20,28},{1,9},{5,13},{9,17},{1... | collective-permute-start | bytes 786440 | tf_op jit(solution)/shard_map/ppermute | solution.py:56
  527.6 22.7 %collective-permute-start.97 = (bf16[128,1024]{1,0:T(8,128)(2,1)}, bf16[128,1024]{1,0:T(8,128)(2,1)}, u32[]{:S(2)}, u32[]{:S(2)}) collective-permute-start(bf16[128,1024]{1,0:T(8,128)(2,1)} %get-tuple-element.56), channel_id=1, source_target_pairs={{8,0},{12,4},{16,8},{20,12},{24,16},{28,20},{9,1},{13,5},{17,9},{2... | collective-permute-start | bytes 786440 | tf_op jit(solution)/shard_map/ppermute | solution.py:56
  (96 other events, 961.8 us)
